TPU v7x, 32 devices: a whole 2x2x4 slice. The times are simulated.
32 devices in a mesh: wide: 8 (over z, y), quad: 4 (over x, core).
Axes of the slice: x: 2, y: 2, z: 4, core: 2. Of those that a mesh axis runs over, the one named last changes fastest.
Arguments:
- orbitals: float32 [16, 64, 4096], P('wide', 'quad'), may hold values from -6 to 6
- corners: int32 [16, 2], P('wide'), may hold values from 0 to 16
- pair_partner: int32 [32], P('wide'), may hold values from 0 to 15, as said below
- pair_live: int32 [32], P('wide'), may hold values from 0 to 1, as said below
Outputs:
- exchange_action: float32 [16, 64, 4096], P('wide', 'quad')
Inputs may be any that keep to these rules, and one draw needn't show every extreme that they name: For the slots of owner w, the second orbital lies between the first plus 1 and the first plus 4 where the slot is live; every pair_partner is a valid orbital index. The number of live slots differs from owner to owner, and owner 0 has all 4 live. `pair_live`: dead slots may stand anywhere among an owner's slots.
All inputs are finite; a program needn't handle non-finite values.
Results may differ from a plain program's by a relative error of at most 0.0003.
Values sent between devices are 32-bit elements; how exact they have to be, the bound alone decides.
A program may use at most 64 MiB of HBM per device.

v0:
```python
import math

import jax
import jax.numpy as jnp
from jax import lax
from jax.sharding import PartitionSpec as P

BZ = 64
SPAN = 16
SWEEPS = 8


def padded_2(block, sides, width):
    for axis, dim in sides:
        count = lax.axis_size(axis)
        forward = [(i, i + 1) for i in range(count - 1)]
        backward = [(target, source) for source, target in forward]
        low = lax.ppermute(
            lax.slice_in_dim(block, block.shape[dim] - width, None, axis=dim), axis, forward
        )
        high = lax.ppermute(lax.slice_in_dim(block, 0, width, axis=dim), axis, backward)
        block = jnp.concatenate([low, block, high], axis=dim)
    return block


def passed_along(x, axis, by):
    size = lax.axis_size(axis)
    pairs = [(i, i + by) for i in range(size) if 0 <= i + by < size]
    return lax.ppermute(x, axis, pairs)


def sweep_weights():
    low = 0.5 / 6.5
    high = 12.5 / 6.5
    center = (high + low) / 2.0
    half = (high - low) / 2.0
    return [
        1.0 / (center + half * math.cos(math.pi * (2 * k + 1) / (2 * SWEEPS)))
        for k in range(SWEEPS)
    ]


def move_box(box, shift_y, shift_z):
    margin = SPAN * BZ + SPAN
    flat = box.shape[-1]
    padded = jnp.pad(box, ((0, 0), (margin, margin)))
    start = margin - shift_y * BZ - shift_z
    taken = lax.dynamic_slice_in_dim(padded, start, flat, 1)
    source = jnp.arange(flat, dtype=jnp.int32) % BZ - shift_z
    keep = (source >= 0) & (source < BZ)
    return jnp.where(keep[None, :], taken, jnp.zeros_like(taken))


def neighbours(field, padded):
    flat = field.shape[-1]
    zpos = jnp.arange(flat, dtype=jnp.int32) % BZ
    total = padded[:, 2:] + padded[:, :-2]
    upper_z = jnp.pad(field[..., 1:], ((0, 0), (0, 0), (0, 1)))
    lower_z = jnp.pad(field[..., :-1], ((0, 0), (0, 0), (1, 0)))
    total = total + jnp.where(zpos < BZ - 1, upper_z, 0.0) + jnp.where(zpos > 0, lower_z, 0.0)
    total = total + jnp.pad(field[..., BZ:], ((0, 0), (0, 0), (0, BZ)))
    total = total + jnp.pad(field[..., :-BZ], ((0, 0), (0, 0), (BZ, 0)))
    return total


def solve_slabs(density):
    weights = sweep_weights()
    potential = weights[0] * density / 6.5
    for k in range(1, SWEEPS):
        padded = padded_2(potential, (("quad", 1),), 1)
        applied = 6.5 * potential - neighbours(potential, padded)
        potential = potential + weights[k] * (density - applied) / 6.5
    return potential


def per_device(orbitals, corners, pair_partner, pair_live):
    per_owner = orbitals.shape[0]
    slot_count = pair_partner.shape[0]
    base = lax.axis_index("wide") * per_owner
    corner_float = corners.astype(jnp.float32)
    pool_orbs = [orbitals]
    pool_corners = [corner_float]
    for step in range(1, 3):
        ahead, ahead_corners = passed_along((orbitals, corner_float), "wide", -step)
        pool_orbs.append(ahead)
        pool_corners.append(ahead_corners)
    pool = jnp.concatenate(pool_orbs, axis=0)
    pool_corner = jnp.concatenate(pool_corners, axis=0).astype(jnp.int32)
    width = pool.shape[0]
    left_index = jnp.arange(slot_count, dtype=jnp.int32) % per_owner
    right_index = jnp.clip(pair_partner - base, 0, width - 1)
    own = orbitals[left_index]
    offset = pool_corner[right_index] - corners[left_index]
    moved = jax.vmap(move_box)(pool[right_index], offset[:, 0], offset[:, 1])
    density = own * moved * pair_live.astype(jnp.float32)[:, None, None]
    potential = solve_slabs(density)
    left_terms = potential * moved
    right_terms = jax.vmap(move_box)(potential * own, -offset[:, 0], -offset[:, 1])
    rows = jnp.arange(width, dtype=jnp.int32)[:, None]
    left_table = (rows == left_index[None, :]).astype(jnp.float32)
    right_table = (rows == right_index[None, :]).astype(jnp.float32)
    gathered = jnp.einsum("op,pxf->oxf", left_table, left_terms, precision=lax.Precision.HIGHEST)
    gathered = gathered + jnp.einsum(
        "op,pxf->oxf", right_table, right_terms, precision=lax.Precision.HIGHEST
    )
    result = gathered[:per_owner]
    for step in range(1, 3):
        segment = gathered[step * per_owner : (step + 1) * per_owner]
        result = result + passed_along(segment, "wide", step)
    return result


def solution(mesh):
    in_specs = (P("wide", "quad", None), P("wide", None), P("wide"), P("wide"))
    out_specs = P("wide", "quad", None)
    return jax.shard_map(
        per_device, mesh=mesh, in_specs=in_specs, out_specs=out_specs, check_vma=False
    )
```

profile of v0, /device:TPU:13, one launch (start us, length us, event | category | flops | bytes accessed | tf_op | source)
XLA Modules:
  0.0 158.0 jit_solution(6380533826490439549)
XLA Ops:
  0.0 0.8 copy.11
  0.8 2.1 %collective-permute-start = (f32[2,2]{0,1:T(2,128)S(1)}, f32[2,2]{0,1:T(2,128)S(1)}, u32[]{:S(2)}, u32[]{:S(2)}) collective-permute-start(f32[2,2]{0,1:T(2,128)S(1)} %convert_element_type.46), channel_id=1, source_target_pairs={{4,0},{8,4},{12,8},{16,12},{20,16},{24,20},{28,24},{5,1},{9,5},{13... | collective-permute-start | bytes 56 | tf_op jit(solution)/shard_map/ppermute | solution.py:29
  3.0 1.9 %collective-permute-start.1 = (f32[2,2]{0,1:T(2,128)S(1)}, f32[2,2]{0,1:T(2,128)S(1)}, u32[]{:S(2)}, u32[]{:S(2)}) collective-permute-start(f32[2,2]{0,1:T(2,128)S(1)} %convert_element_type.46), channel_id=1, source_target_pairs={{8,0},{12,4},{16,8},{20,12},{24,16},{28,20},{9,1},{13,5},{17,9},{2... | collective-permute-start | bytes 56 | tf_op jit(solution)/shard_map/ppermute | solution.py:29
  4.9 3.0 %collective-permute-start.2 = (f32[2,16,4096]{2,1,0:T(8,128)}, f32[2,16,4096]{2,1,0:T(8,128)S(1)}, u32[]{:S(2)}, u32[]{:S(2)}) collective-permute-start(f32[2,16,4096]{2,1,0:T(8,128)} %param.4), channel_id=1, source_target_pairs={{4,0},{8,4},{12,8},{16,12},{20,16},{24,20},{28,24},{5,1},{9,5},{13... | collective-permute-start | bytes 1572872 | tf_op jit(solution)/shard_map/ppermute | solution.py:29
  7.9 1.9 %collective-permute-start.3 = (f32[2,16,4096]{2,1,0:T(8,128)}, f32[2,16,4096]{2,1,0:T(8,128)S(1)}, u32[]{:S(2)}, u32[]{:S(2)}) collective-permute-start(f32[2,16,4096]{2,1,0:T(8,128)} %param.4), channel_id=1, source_target_pairs={{8,0},{12,4},{16,8},{20,12},{24,16},{28,20},{9,1},{13,5},{17,9},{2... | collective-permute-start | bytes 1572872 | tf_op jit(solution)/shard_map/ppermute | solution.py:29
  10.0 1.2 gather_fusion.2
  11.3 1.7 %gather_fusion = f32[4,16,4096]{2,1,0:T(8,128)S(1)} fusion(f32[2,16,4096]{2,1,0:T(8,128)} %param.4, s32[1024]{0:T(1024)S(1)} %pad_clamp_fusion.1), kind=kCustom, calls=%fused_computation | custom fusion | bytes 2097168 | tf_op jit(solution)/shard_map/gather | solution.py:92
  14.2 6.2 %collective-permute-done.2 = f32[2,16,4096]{2,1,0:T(8,128)S(1)} collective-permute-done((f32[2,16,4096]{2,1,0:T(8,128)}, f32[2,16,4096]{2,1,0:T(8,128)S(1)}, u32[]{:S(2)}, u32[]{:S(2)}) %collective-permute-start.2) | collective-permute-done | bytes 524320 | tf_op jit(solution)/shard_map/ppermute | solution.py:29
  20.4 1.8 %collective-permute-done.3 = f32[2,16,4096]{2,1,0:T(8,128)S(1)} collective-permute-done((f32[2,16,4096]{2,1,0:T(8,128)}, f32[2,16,4096]{2,1,0:T(8,128)S(1)}, u32[]{:S(2)}, u32[]{:S(2)}) %collective-permute-start.3) | collective-permute-done | bytes 524320 | tf_op jit(solution)/shard_map/ppermute | solution.py:29
  22.2 1.3 pad_maximum_fusion
  23.5 2.0 %gather_fusion.3 = f32[4,16,4096]{2,1,0:T(8,128)S(1)} fusion(f32[6,16,4096]{2,1,0:T(8,128)} %pad_maximum_fusion, s32[1024]{0:T(1024)S(1)} %pad_clamp_fusion), kind=kCustom, calls=%fused_computation.3 | custom fusion | bytes 2097168 | tf_op jit(solution)/shard_map/gather | solution.py:94
  25.5 1.6 pad.97
  27.2 11.8 %while.2 = (s32[]{:T(128)}, f32[4,16,6176]{2,1,0:T(8,128)}, s32[4,3]{1,0:T(4,128)S(1)}, f32[4,16,4096]{2,1,0:T(8,128)S(1)}, s32[]{:T(128)}) while((s32[]{:T(128)}, f32[4,16,6176]{2,1,0:T(8,128)}, s32[4,3]{1,0:T(4,128)S(1)}, f32[4,16,4096]{2,1,0:T(8,128)S(1)}, s32[]{:T(128)}) %tuple.65), condition=%wide.while_cond, body=%wide.while_body.sunk | while | flops 2 | bytes 524405 | solution.py:48
  27.2 0.6 fusion.110
  27.8 2.3 %dynamic-slice_dynamic-update-slice_fusion.4 = f32[4,16,4096]{2,1,0:T(8,128)S(1)} fusion(f32[4,16,4096]{2,1,0:T(8,128)S(1)} %get-tuple-element.169, s32[]{:T(128)} %get-tuple-element.166, f32[4,16,6176]{2,1,0:T(8,128)} %get-tuple-element.172, s32[]{:T(128)} %bitcast.14, s32[]{:T(128)} %bitcast.15), kind=kLoop, calls=%fused_computation.4.clone.1 | loop fusion | bytes 524300 | tf_op jit(solution)/shard_map/vmap()/gather
  30.7 2.3 %dynamic-slice_dynamic-update-slice_fusion.4 = f32[4,16,4096]{2,1,0:T(8,128)S(1)} fusion(f32[4,16,4096]{2,1,0:T(8,128)S(1)} %get-tuple-element.169, s32[]{:T(128)} %get-tuple-element.166, f32[4,16,6176]{2,1,0:T(8,128)} %get-tuple-element.172, s32[]{:T(128)} %bitcast.14, s32[]{:T(128)} %bitcast.15), kind=kLoop, calls=%fused_computation.4.clone.1 | loop fusion | bytes 524300 | tf_op jit(solution)/shard_map/vmap()/gather
  33.7 2.3 %dynamic-slice_dynamic-update-slice_fusion.4 = f32[4,16,4096]{2,1,0:T(8,128)S(1)} fusion(f32[4,16,4096]{2,1,0:T(8,128)S(1)} %get-tuple-element.169, s32[]{:T(128)} %get-tuple-element.166, f32[4,16,6176]{2,1,0:T(8,128)} %get-tuple-element.172, s32[]{:T(128)} %bitcast.14, s32[]{:T(128)} %bitcast.15), kind=kLoop, calls=%fused_computation.4.clone.1 | loop fusion | bytes 524300 | tf_op jit(solution)/shard_map/vmap()/gather
  36.6 2.3 %dynamic-slice_dynamic-update-slice_fusion.4 = f32[4,16,4096]{2,1,0:T(8,128)S(1)} fusion(f32[4,16,4096]{2,1,0:T(8,128)S(1)} %get-tuple-element.169, s32[]{:T(128)} %get-tuple-element.166, f32[4,16,6176]{2,1,0:T(8,128)} %get-tuple-element.172, s32[]{:T(128)} %bitcast.14, s32[]{:T(128)} %bitcast.15), kind=kLoop, calls=%fused_computation.4.clone.1 | loop fusion | bytes 524300 | tf_op jit(solution)/shard_map/vmap()/gather
  39.7 4.1 %collective-permute-start.4 = (f32[4,1,4096]{2,1,0:T(1,128)S(1)}, f32[4,1,4096]{2,1,0:T(1,128)S(1)}, u32[]{:S(2)}, u32[]{:S(2)}) collective-permute-start(f32[4,1,4096]{2,1,0:T(1,128)S(1)} %get-tuple-element.91), channel_id=1, source_target_pairs={{1,0},{2,1},{3,2},{5,4},{6,5},{7,6},{9,8},{10,9},{11,10},{13,12},{... | collective-permute-start | bytes 196616 | tf_op jit(solution)/shard_map/ppermute | solution.py:21
  43.8 3.0 %collective-permute-start.5 = (f32[4,1,4096]{2,1,0:T(1,128)S(1)}, f32[4,1,4096]{2,1,0:T(1,128)S(1)}, u32[]{:S(2)}, u32[]{:S(2)}) collective-permute-start(f32[4,1,4096]{2,1,0:T(1,128)S(1)} %get-tuple-element.92), channel_id=1, source_target_pairs={{0,1},{1,2},{2,3},{4,5},{5,6},{6,7},{8,9},{9,10},{10,11},{12,13},{... | collective-permute-start | bytes 196616 | tf_op jit(solution)/shard_map/ppermute | solution.py:18
  47.2 0.9 collective-permute-done.5
  48.1 1.0 fusion.62
  49.5 1.9 %collective-permute-start.6 = (f32[4,1,4096]{2,1,0:T(1,128)S(1)}, f32[4,1,4096]{2,1,0:T(1,128)S(1)}, u32[]{:S(2)}, u32[]{:S(2)}) collective-permute-start(f32[4,1,4096]{2,1,0:T(1,128)S(1)} %get-tuple-element.85), channel_id=1, source_target_pairs={{1,0},{2,1},{3,2},{5,4},{6,5},{7,6},{9,8},{10,9},{11,10},{13,12},{... | collective-permute-start | bytes 196616 | tf_op jit(solution)/shard_map/ppermute | solution.py:21
  51.5 4.3 %collective-permute-start.7 = (f32[4,1,4096]{2,1,0:T(1,128)S(1)}, f32[4,1,4096]{2,1,0:T(1,128)S(1)}, u32[]{:S(2)}, u32[]{:S(2)}) collective-permute-start(f32[4,1,4096]{2,1,0:T(1,128)S(1)} %get-tuple-element.86), channel_id=1, source_target_pairs={{0,1},{1,2},{2,3},{4,5},{5,6},{6,7},{8,9},{9,10},{10,11},{12,13},{... | collective-permute-start | bytes 196616 | tf_op jit(solution)/shard_map/ppermute | solution.py:18
  56.1 0.9 collective-permute-done.7
  57.1 0.9 fusion.53
  58.4 1.9 %collective-permute-start.8 = (f32[4,1,4096]{2,1,0:T(1,128)S(1)}, f32[4,1,4096]{2,1,0:T(1,128)S(1)}, u32[]{:S(2)}, u32[]{:S(2)}) collective-permute-start(f32[4,1,4096]{2,1,0:T(1,128)S(1)} %get-tuple-element.79), channel_id=1, source_target_pairs={{1,0},{2,1},{3,2},{5,4},{6,5},{7,6},{9,8},{10,9},{11,10},{13,12},{... | collective-permute-start | bytes 196616 | tf_op jit(solution)/shard_map/ppermute | solution.py:21
  60.4 4.3 %collective-permute-start.9 = (f32[4,1,4096]{2,1,0:T(1,128)S(1)}, f32[4,1,4096]{2,1,0:T(1,128)S(1)}, u32[]{:S(2)}, u32[]{:S(2)}) collective-permute-start(f32[4,1,4096]{2,1,0:T(1,128)S(1)} %get-tuple-element.80), channel_id=1, source_target_pairs={{0,1},{1,2},{2,3},{4,5},{5,6},{6,7},{8,9},{9,10},{10,11},{12,13},{... | collective-permute-start | bytes 196616 | tf_op jit(solution)/shard_map/ppermute | solution.py:18
  65.0 0.9 collective-permute-done.9
  65.9 0.9 fusion.44
  67.3 1.9 %collective-permute-start.10 = (f32[4,1,4096]{2,1,0:T(1,128)S(1)}, f32[4,1,4096]{2,1,0:T(1,128)S(1)}, u32[]{:S(2)}, u32[]{:S(2)}) collective-permute-start(f32[4,1,4096]{2,1,0:T(1,128)S(1)} %get-tuple-element.73), channel_id=1, source_target_pairs={{1,0},{2,1},{3,2},{5,4},{6,5},{7,6},{9,8},{10,9},{11,10},{13,12},{... | collective-permute-start | bytes 196616 | tf_op jit(solution)/shard_map/ppermute | solution.py:21
  69.3 4.3 %collective-permute-start.11 = (f32[4,1,4096]{2,1,0:T(1,128)S(1)}, f32[4,1,4096]{2,1,0:T(1,128)S(1)}, u32[]{:S(2)}, u32[]{:S(2)}) collective-permute-start(f32[4,1,4096]{2,1,0:T(1,128)S(1)} %get-tuple-element.74), channel_id=1, source_target_pairs={{0,1},{1,2},{2,3},{4,5},{5,6},{6,7},{8,9},{9,10},{10,11},{12,13},{... | collective-permute-start | bytes 196616 | tf_op jit(solution)/shard_map/ppermute | solution.py:18
  73.9 0.9 collective-permute-done.11
  74.8 0.9 fusion.35
  76.2 1.9 %collective-permute-start.12 = (f32[4,1,4096]{2,1,0:T(1,128)S(1)}, f32[4,1,4096]{2,1,0:T(1,128)S(1)}, u32[]{:S(2)}, u32[]{:S(2)}) collective-permute-start(f32[4,1,4096]{2,1,0:T(1,128)S(1)} %get-tuple-element.67), channel_id=1, source_target_pairs={{1,0},{2,1},{3,2},{5,4},{6,5},{7,6},{9,8},{10,9},{11,10},{13,12},{... | collective-permute-start | bytes 196616 | tf_op jit(solution)/shard_map/ppermute | solution.py:21
  78.1 4.3 %collective-permute-start.13 = (f32[4,1,4096]{2,1,0:T(1,128)S(1)}, f32[4,1,4096]{2,1,0:T(1,128)S(1)}, u32[]{:S(2)}, u32[]{:S(2)}) collective-permute-start(f32[4,1,4096]{2,1,0:T(1,128)S(1)} %get-tuple-element.68), channel_id=1, source_target_pairs={{0,1},{1,2},{2,3},{4,5},{5,6},{6,7},{8,9},{9,10},{10,11},{12,13},{... | collective-permute-start | bytes 196616 | tf_op jit(solution)/shard_map/ppermute | solution.py:18
  82.8 0.9 collective-permute-done.13
  83.7 0.9 fusion.26
  85.1 1.9 %collective-permute-start.14 = (f32[4,1,4096]{2,1,0:T(1,128)S(1)}, f32[4,1,4096]{2,1,0:T(1,128)S(1)}, u32[]{:S(2)}, u32[]{:S(2)}) collective-permute-start(f32[4,1,4096]{2,1,0:T(1,128)S(1)} %get-tuple-element.61), channel_id=1, source_target_pairs={{1,0},{2,1},{3,2},{5,4},{6,5},{7,6},{9,8},{10,9},{11,10},{13,12},{... | collective-permute-start | bytes 196616 | tf_op jit(solution)/shard_map/ppermute | solution.py:21
  87.0 4.4 %collective-permute-start.15 = (f32[4,1,4096]{2,1,0:T(1,128)S(1)}, f32[4,1,4096]{2,1,0:T(1,128)S(1)}, u32[]{:S(2)}, u32[]{:S(2)}) collective-permute-start(f32[4,1,4096]{2,1,0:T(1,128)S(1)} %get-tuple-element.62), channel_id=1, source_target_pairs={{0,1},{1,2},{2,3},{4,5},{5,6},{6,7},{8,9},{9,10},{10,11},{12,13},{... | collective-permute-start | bytes 196616 | tf_op jit(solution)/shard_map/ppermute | solution.py:18
  91.9 0.8 collective-permute-done.15
  92.6 0.9 fusion.17
  94.0 1.9 %collective-permute-start.16 = (f32[4,1,4096]{2,1,0:T(1,128)S(1)}, f32[4,1,4096]{2,1,0:T(1,128)S(1)}, u32[]{:S(2)}, u32[]{:S(2)}) collective-permute-start(f32[4,1,4096]{2,1,0:T(1,128)S(1)} %get-tuple-element.51), channel_id=1, source_target_pairs={{1,0},{2,1},{3,2},{5,4},{6,5},{7,6},{9,8},{10,9},{11,10},{13,12},{... | collective-permute-start | bytes 196616 | tf_op jit(solution)/shard_map/ppermute | solution.py:21
  95.9 4.3 %collective-permute-start.17 = (f32[4,1,4096]{2,1,0:T(1,128)S(1)}, f32[4,1,4096]{2,1,0:T(1,128)S(1)}, u32[]{:S(2)}, u32[]{:S(2)}) collective-permute-start(f32[4,1,4096]{2,1,0:T(1,128)S(1)} %get-tuple-element.52), channel_id=1, source_target_pairs={{0,1},{1,2},{2,3},{4,5},{5,6},{6,7},{8,9},{9,10},{10,11},{12,13},{... | collective-permute-start | bytes 196616 | tf_op jit(solution)/shard_map/ppermute | solution.py:18
  100.6 0.9 collective-permute-done.17
  101.5 2.0 %fusion.82 = (f32[4,16,4096]{2,1,0:T(8,128)S(1)}, f32[4,16,4096]{2,1,0:T(8,128)}) fusion(f32[4,16,4096]{2,1,0:T(8,128)S(1)} %gather_fusion, f32[4,16,4096]{2,1,0:T(8,128)S(1)} %fusion.17, f32[4,16,4096]{2,1,0:T(8,128)S(1)} %get-tuple-element.42, f32[4,16,4032]{2,1,0:T(8,128)S(1)} %get-tuple-element.56, f32[4,16,4032]{2,1,0:T(8,128)S(1)} %get-tuple-element.55, ...), kind=kLoop, calls=%fused_computation.134 | loop fusion | flops 3932160 | bytes 9543168 | tf_op jit(solution)/shard_map/mul | solution.py:98
  103.8 1.1 broadcast.271
  104.9 10.9 %while.3 = (s32[]{:T(128)}, f32[4,16,6176]{2,1,0:T(8,128)S(1)}, s32[4,3]{1,0:T(4,128)S(1)}, f32[4,16,4096]{2,1,0:T(8,128)}, s32[]{:T(128)}) while((s32[]{:T(128)}, f32[4,16,6176]{2,1,0:T(8,128)S(1)}, s32[4,3]{1,0:T(4,128)S(1)}, f32[4,16,4096]{2,1,0:T(8,128)}, s32[]{:T(128)}) %tuple.68), condition=%wide.while_cond.1, body=%wide.while_body.1.sunk | while | flops 2 | bytes 525929 | solution.py:48
  104.9 0.6 fusion.111
  105.5 2.1 %dynamic-slice_dynamic-update-slice_fusion.5 = f32[4,16,4096]{2,1,0:T(8,128)} fusion(f32[4,16,4096]{2,1,0:T(8,128)} %get-tuple-element.184, s32[]{:T(128)} %get-tuple-element.181, f32[4,16,6176]{2,1,0:T(8,128)S(1)} %get-tuple-element.187, s32[]{:T(128)} %bitcast.16, s32[]{:T(128)} %bitcast.17), kind=kLoop, calls=%fused_computation.6.clone.1 | loop fusion | bytes 525824 | tf_op jit(solution)/shard_map/vmap()/gather
  107.6 0.6 fusion.111
  108.3 2.1 %dynamic-slice_dynamic-update-slice_fusion.5 = f32[4,16,4096]{2,1,0:T(8,128)} fusion(f32[4,16,4096]{2,1,0:T(8,128)} %get-tuple-element.184, s32[]{:T(128)} %get-tuple-element.181, f32[4,16,6176]{2,1,0:T(8,128)S(1)} %get-tuple-element.187, s32[]{:T(128)} %bitcast.16, s32[]{:T(128)} %bitcast.17), kind=kLoop, calls=%fused_computation.6.clone.1 | loop fusion | bytes 525824 | tf_op jit(solution)/shard_map/vmap()/gather
  110.4 0.6 fusion.111
  111.0 2.1 %dynamic-slice_dynamic-update-slice_fusion.5 = f32[4,16,4096]{2,1,0:T(8,128)} fusion(f32[4,16,4096]{2,1,0:T(8,128)} %get-tuple-element.184, s32[]{:T(128)} %get-tuple-element.181, f32[4,16,6176]{2,1,0:T(8,128)S(1)} %get-tuple-element.187, s32[]{:T(128)} %bitcast.16, s32[]{:T(128)} %bitcast.17), kind=kLoop, calls=%fused_computation.6.clone.1 | loop fusion | bytes 525824 | tf_op jit(solution)/shard_map/vmap()/gather
  113.1 0.6 fusion.111
  113.8 2.1 %dynamic-slice_dynamic-update-slice_fusion.5 = f32[4,16,4096]{2,1,0:T(8,128)} fusion(f32[4,16,4096]{2,1,0:T(8,128)} %get-tuple-element.184, s32[]{:T(128)} %get-tuple-element.181, f32[4,16,6176]{2,1,0:T(8,128)S(1)} %get-tuple-element.187, s32[]{:T(128)} %bitcast.16, s32[]{:T(128)} %bitcast.17), kind=kLoop, calls=%fused_computation.6.clone.1 | loop fusion | bytes 525824 | tf_op jit(solution)/shard_map/vmap()/gather
  115.8 1.8 %select_multiply_fusion = (f32[4,16,4096]{2,1,0:T(8,128)S(1)}, f32[4,16,4096]{2,1,0:T(8,128)S(1)}) fusion(f32[4,16,4096]{2,1,0:T(8,128)} %get-tuple-element.40, f32[4,16,4096]{2,1,0:T(8,128)S(1)} %get-tuple-element.12, pred[4,4096]{1,0:T(4,128)(4,1)S(1)} %get-tuple-element.94, f32[4,16,4096]{2,1,0:T(8,128)} %get-tuple-element.20, ...), kind=kLoop, calls=%fused_computation.91 | loop fusion | flops 786432 | bytes 5275648 | tf_op jit(solution)/shard_map/mul | solution.py:97
  117.7 1.9 %fusion.64 = f32[6,16,4096]{2,0,1:T(8,128)S(1)} fusion(f32[4,16,4096]{2,1,0:T(8,128)S(1)} %get-tuple-element.101, s32[4]{0:T(128)S(1)} %and_select_fusion), kind=kOutput, calls=%fused_computation.88 | convolution fusion | flops 18874392 | bytes 2621456 | tf_op jit(solution)/shard_map/op,pxf->oxf/dot_general | solution.py:102
  119.6 2.1 %convolution_add_fusion = f32[6,16,4096]{2,0,1:T(8,128)S(1)} fusion(f32[6,16,4096]{2,0,1:T(8,128)S(1)} %fusion.64, f32[4,16,4096]{2,1,0:T(8,128)S(1)} %get-tuple-element.102, s32[4]{0:T(128)S(1)} %get-tuple-element.44), kind=kOutput, calls=%fused_computation.8 | convolution fusion | flops 19267608 | bytes 4194320 | tf_op jit(solution)/shard_map/op,pxf->oxf/dot_general | solution.py:103
  122.2 12.5 %collective-permute-start.18 = (f32[2,16,4096]{2,0,1:T(2,128)S(1)}, f32[2,16,4096]{2,0,1:T(2,128)S(1)}, u32[]{:S(2)}, u32[]{:S(2)}) collective-permute-start(f32[2,16,4096]{2,0,1:T(2,128)S(1)} %get-tuple-element.49), channel_id=1, source_target_pairs={{0,4},{4,8},{8,12},{12,16},{16,20},{20,24},{24,28},{1,5},{5,9},{9,... | collective-permute-start | bytes 1572872 | tf_op jit(solution)/shard_map/ppermute | solution.py:29
  134.7 1.9 %collective-permute-start.19 = (f32[2,16,4096]{2,0,1:T(2,128)S(1)}, f32[2,16,4096]{2,0,1:T(2,128)S(1)}, u32[]{:S(2)}, u32[]{:S(2)}) collective-permute-start(f32[2,16,4096]{2,0,1:T(2,128)S(1)} %get-tuple-element.50), channel_id=1, source_target_pairs={{0,8},{4,12},{8,16},{12,20},{16,24},{20,28},{1,9},{5,13},{9,17},{1... | collective-permute-start | bytes 1572872 | tf_op jit(solution)/shard_map/ppermute | solution.py:29
  136.6 9.9 %collective-permute-done.18 = f32[2,16,4096]{2,0,1:T(2,128)S(1)} collective-permute-done((f32[2,16,4096]{2,0,1:T(2,128)S(1)}, f32[2,16,4096]{2,0,1:T(2,128)S(1)}, u32[]{:S(2)}, u32[]{:S(2)}) %collective-permute-start.18) | collective-permute-done | bytes 524320 | tf_op jit(solution)/shard_map/ppermute | solution.py:29
  146.5 10.0 %collective-permute-done.19 = f32[2,16,4096]{2,0,1:T(2,128)S(1)} collective-permute-done((f32[2,16,4096]{2,0,1:T(2,128)S(1)}, f32[2,16,4096]{2,0,1:T(2,128)S(1)}, u32[]{:S(2)}, u32[]{:S(2)}) %collective-permute-start.19) | collective-permute-done | bytes 524320 | tf_op jit(solution)/shard_map/ppermute | solution.py:29
  156.9 1.1 copy.15
  (71 shorter events, 10.4 us)
Async XLA Ops:
  0.0 22.2 %copy-start = (f32[2,16,4096]{2,1,0:T(8,128)S(1)}, f32[2,16,4096]{2,1,0:T(8,128)}, u32[]{:S(2)}) copy-start(f32[2,16,4096]{2,1,0:T(8,128)} %param.4) | copy-start | bytes 1572868
  0.0 13.0 %copy-start.1 = (s32[4]{0:T(128)S(1)}, s32[4]{0:T(128)}, u32[]{:S(2)}) copy-start(s32[4]{0:T(128)} %param.6) | copy-start | bytes 52
  0.0 13.0 %copy-start.2 = (s32[4]{0:T(128)S(1)}, s32[4]{0:T(128)}, u32[]{:S(2)}) copy-start(s32[4]{0:T(128)} %param.7) | copy-start | bytes 52
  0.8 12.2 %collective-permute-start = (f32[2,2]{0,1:T(2,128)S(1)}, f32[2,2]{0,1:T(2,128)S(1)}, u32[]{:S(2)}, u32[]{:S(2)}) collective-permute-start(f32[2,2]{0,1:T(2,128)S(1)} %convert_element_type.46), channel_id=1, source_target_pairs={{4,0},{8,4},{12,8},{16,12},{20,16},{24,20},{28,24},{5,1},{9,5},{13... | collective-permute-start | bytes 56 | tf_op jit(solution)/shard_map/ppermute | solution.py:29
  3.0 10.1 %collective-permute-start.1 = (f32[2,2]{0,1:T(2,128)S(1)}, f32[2,2]{0,1:T(2,128)S(1)}, u32[]{:S(2)}, u32[]{:S(2)}) collective-permute-start(f32[2,2]{0,1:T(2,128)S(1)} %convert_element_type.46), channel_id=1, source_target_pairs={{8,0},{12,4},{16,8},{20,12},{24,16},{28,20},{9,1},{13,5},{17,9},{2... | collective-permute-start | bytes 56 | tf_op jit(solution)/shard_map/ppermute | solution.py:29
  4.9 15.5 %collective-permute-start.2 = (f32[2,16,4096]{2,1,0:T(8,128)}, f32[2,16,4096]{2,1,0:T(8,128)S(1)}, u32[]{:S(2)}, u32[]{:S(2)}) collective-permute-start(f32[2,16,4096]{2,1,0:T(8,128)} %param.4), channel_id=1, source_target_pairs={{4,0},{8,4},{12,8},{16,12},{20,16},{24,20},{28,24},{5,1},{9,5},{13... | collective-permute-start | bytes 1572872 | tf_op jit(solution)/shard_map/ppermute | solution.py:29
  7.9 14.3 %collective-permute-start.3 = (f32[2,16,4096]{2,1,0:T(8,128)}, f32[2,16,4096]{2,1,0:T(8,128)S(1)}, u32[]{:S(2)}, u32[]{:S(2)}) collective-permute-start(f32[2,16,4096]{2,1,0:T(8,128)} %param.4), channel_id=1, source_target_pairs={{8,0},{12,4},{16,8},{20,12},{24,16},{28,20},{9,1},{13,5},{17,9},{2... | collective-permute-start | bytes 1572872 | tf_op jit(solution)/shard_map/ppermute | solution.py:29
  39.7 7.5 %collective-permute-start.4 = (f32[4,1,4096]{2,1,0:T(1,128)S(1)}, f32[4,1,4096]{2,1,0:T(1,128)S(1)}, u32[]{:S(2)}, u32[]{:S(2)}) collective-permute-start(f32[4,1,4096]{2,1,0:T(1,128)S(1)} %get-tuple-element.91), channel_id=1, source_target_pairs={{1,0},{2,1},{3,2},{5,4},{6,5},{7,6},{9,8},{10,9},{11,10},{13,12},{... | collective-permute-start | bytes 196616 | tf_op jit(solution)/shard_map/ppermute | solution.py:21
  43.8 4.3 %collective-permute-start.5 = (f32[4,1,4096]{2,1,0:T(1,128)S(1)}, f32[4,1,4096]{2,1,0:T(1,128)S(1)}, u32[]{:S(2)}, u32[]{:S(2)}) collective-permute-start(f32[4,1,4096]{2,1,0:T(1,128)S(1)} %get-tuple-element.92), channel_id=1, source_target_pairs={{0,1},{1,2},{2,3},{4,5},{5,6},{6,7},{8,9},{9,10},{10,11},{12,13},{... | collective-permute-start | bytes 196616 | tf_op jit(solution)/shard_map/ppermute | solution.py:18
  49.5 6.6 %collective-permute-start.6 = (f32[4,1,4096]{2,1,0:T(1,128)S(1)}, f32[4,1,4096]{2,1,0:T(1,128)S(1)}, u32[]{:S(2)}, u32[]{:S(2)}) collective-permute-start(f32[4,1,4096]{2,1,0:T(1,128)S(1)} %get-tuple-element.85), channel_id=1, source_target_pairs={{1,0},{2,1},{3,2},{5,4},{6,5},{7,6},{9,8},{10,9},{11,10},{13,12},{... | collective-permute-start | bytes 196616 | tf_op jit(solution)/shard_map/ppermute | solution.py:21
  51.5 5.6 %collective-permute-start.7 = (f32[4,1,4096]{2,1,0:T(1,128)S(1)}, f32[4,1,4096]{2,1,0:T(1,128)S(1)}, u32[]{:S(2)}, u32[]{:S(2)}) collective-permute-start(f32[4,1,4096]{2,1,0:T(1,128)S(1)} %get-tuple-element.86), channel_id=1, source_target_pairs={{0,1},{1,2},{2,3},{4,5},{5,6},{6,7},{8,9},{9,10},{10,11},{12,13},{... | collective-permute-start | bytes 196616 | tf_op jit(solution)/shard_map/ppermute | solution.py:18
  58.4 6.6 %collective-permute-start.8 = (f32[4,1,4096]{2,1,0:T(1,128)S(1)}, f32[4,1,4096]{2,1,0:T(1,128)S(1)}, u32[]{:S(2)}, u32[]{:S(2)}) collective-permute-start(f32[4,1,4096]{2,1,0:T(1,128)S(1)} %get-tuple-element.79), channel_id=1, source_target_pairs={{1,0},{2,1},{3,2},{5,4},{6,5},{7,6},{9,8},{10,9},{11,10},{13,12},{... | collective-permute-start | bytes 196616 | tf_op jit(solution)/shard_map/ppermute | solution.py:21
  60.4 5.6 %collective-permute-start.9 = (f32[4,1,4096]{2,1,0:T(1,128)S(1)}, f32[4,1,4096]{2,1,0:T(1,128)S(1)}, u32[]{:S(2)}, u32[]{:S(2)}) collective-permute-start(f32[4,1,4096]{2,1,0:T(1,128)S(1)} %get-tuple-element.80), channel_id=1, source_target_pairs={{0,1},{1,2},{2,3},{4,5},{5,6},{6,7},{8,9},{9,10},{10,11},{12,13},{... | collective-permute-start | bytes 196616 | tf_op jit(solution)/shard_map/ppermute | solution.py:18
  67.3 6.6 %collective-permute-start.10 = (f32[4,1,4096]{2,1,0:T(1,128)S(1)}, f32[4,1,4096]{2,1,0:T(1,128)S(1)}, u32[]{:S(2)}, u32[]{:S(2)}) collective-permute-start(f32[4,1,4096]{2,1,0:T(1,128)S(1)} %get-tuple-element.73), channel_id=1, source_target_pairs={{1,0},{2,1},{3,2},{5,4},{6,5},{7,6},{9,8},{10,9},{11,10},{13,12},{... | collective-permute-start | bytes 196616 | tf_op jit(solution)/shard_map/ppermute | solution.py:21
  69.3 5.6 %collective-permute-start.11 = (f32[4,1,4096]{2,1,0:T(1,128)S(1)}, f32[4,1,4096]{2,1,0:T(1,128)S(1)}, u32[]{:S(2)}, u32[]{:S(2)}) collective-permute-start(f32[4,1,4096]{2,1,0:T(1,128)S(1)} %get-tuple-element.74), channel_id=1, source_target_pairs={{0,1},{1,2},{2,3},{4,5},{5,6},{6,7},{8,9},{9,10},{10,11},{12,13},{... | collective-permute-start | bytes 196616 | tf_op jit(solution)/shard_map/ppermute | solution.py:18
  76.2 6.6 %collective-permute-start.12 = (f32[4,1,4096]{2,1,0:T(1,128)S(1)}, f32[4,1,4096]{2,1,0:T(1,128)S(1)}, u32[]{:S(2)}, u32[]{:S(2)}) collective-permute-start(f32[4,1,4096]{2,1,0:T(1,128)S(1)} %get-tuple-element.67), channel_id=1, source_target_pairs={{1,0},{2,1},{3,2},{5,4},{6,5},{7,6},{9,8},{10,9},{11,10},{13,12},{... | collective-permute-start | bytes 196616 | tf_op jit(solution)/shard_map/ppermute | solution.py:21
  78.1 5.6 %collective-permute-start.13 = (f32[4,1,4096]{2,1,0:T(1,128)S(1)}, f32[4,1,4096]{2,1,0:T(1,128)S(1)}, u32[]{:S(2)}, u32[]{:S(2)}) collective-permute-start(f32[4,1,4096]{2,1,0:T(1,128)S(1)} %get-tuple-element.68), channel_id=1, source_target_pairs={{0,1},{1,2},{2,3},{4,5},{5,6},{6,7},{8,9},{9,10},{10,11},{12,13},{... | collective-permute-start | bytes 196616 | tf_op jit(solution)/shard_map/ppermute | solution.py:18
  85.1 6.7 %collective-permute-start.14 = (f32[4,1,4096]{2,1,0:T(1,128)S(1)}, f32[4,1,4096]{2,1,0:T(1,128)S(1)}, u32[]{:S(2)}, u32[]{:S(2)}) collective-permute-start(f32[4,1,4096]{2,1,0:T(1,128)S(1)} %get-tuple-element.61), channel_id=1, source_target_pairs={{1,0},{2,1},{3,2},{5,4},{6,5},{7,6},{9,8},{10,9},{11,10},{13,12},{... | collective-permute-start | bytes 196616 | tf_op jit(solution)/shard_map/ppermute | solution.py:21
  87.0 5.6 %collective-permute-start.15 = (f32[4,1,4096]{2,1,0:T(1,128)S(1)}, f32[4,1,4096]{2,1,0:T(1,128)S(1)}, u32[]{:S(2)}, u32[]{:S(2)}) collective-permute-start(f32[4,1,4096]{2,1,0:T(1,128)S(1)} %get-tuple-element.62), channel_id=1, source_target_pairs={{0,1},{1,2},{2,3},{4,5},{5,6},{6,7},{8,9},{9,10},{10,11},{12,13},{... | collective-permute-start | bytes 196616 | tf_op jit(solution)/shard_map/ppermute | solution.py:18
  94.0 6.6 %collective-permute-start.16 = (f32[4,1,4096]{2,1,0:T(1,128)S(1)}, f32[4,1,4096]{2,1,0:T(1,128)S(1)}, u32[]{:S(2)}, u32[]{:S(2)}) collective-permute-start(f32[4,1,4096]{2,1,0:T(1,128)S(1)} %get-tuple-element.51), channel_id=1, source_target_pairs={{1,0},{2,1},{3,2},{5,4},{6,5},{7,6},{9,8},{10,9},{11,10},{13,12},{... | collective-permute-start | bytes 196616 | tf_op jit(solution)/shard_map/ppermute | solution.py:21
  95.9 5.6 %collective-permute-start.17 = (f32[4,1,4096]{2,1,0:T(1,128)S(1)}, f32[4,1,4096]{2,1,0:T(1,128)S(1)}, u32[]{:S(2)}, u32[]{:S(2)}) collective-permute-start(f32[4,1,4096]{2,1,0:T(1,128)S(1)} %get-tuple-element.52), channel_id=1, source_target_pairs={{0,1},{1,2},{2,3},{4,5},{5,6},{6,7},{8,9},{9,10},{10,11},{12,13},{... | collective-permute-start | bytes 196616 | tf_op jit(solution)/shard_map/ppermute | solution.py:18
  122.2 24.2 %collective-permute-start.18 = (f32[2,16,4096]{2,0,1:T(2,128)S(1)}, f32[2,16,4096]{2,0,1:T(2,128)S(1)}, u32[]{:S(2)}, u32[]{:S(2)}) collective-permute-start(f32[2,16,4096]{2,0,1:T(2,128)S(1)} %get-tuple-element.49), channel_id=1, source_target_pairs={{0,4},{4,8},{8,12},{12,16},{16,20},{20,24},{24,28},{1,5},{5,9},{9,... | collective-permute-start | bytes 1572872 | tf_op jit(solution)/shard_map/ppermute | solution.py:29
  134.7 21.7 %collective-permute-start.19 = (f32[2,16,4096]{2,0,1:T(2,128)S(1)}, f32[2,16,4096]{2,0,1:T(2,128)S(1)}, u32[]{:S(2)}, u32[]{:S(2)}) collective-permute-start(f32[2,16,4096]{2,0,1:T(2,128)S(1)} %get-tuple-element.50), channel_id=1, source_target_pairs={{0,8},{4,12},{8,16},{12,20},{16,24},{20,28},{1,9},{5,13},{9,17},{1... | collective-permute-start | bytes 1572872 | tf_op jit(solution)/shard_map/ppermute | solution.py:29
where the time goes:
time: 160 us; the launch traced here: 158 us
  starting transfers between devices  67.8 us (42%)
  local copies, waits for them, and re-layouts  39.3 us (25%)
  waiting for transfers between devices  34.3 us (21%)
  other arithmetic  12 us (8%)
  matrix products  3.96 us (2%)
    ppermute x7, starting transfers between devices, padded_2(): lax.ppermute(lax.slice_in_dim(block, block.shape[dim] - width, None, axis...  28.8 us
    ppermute x6, waiting for transfers between devices, passed_along(): return lax.ppermute(x, axis, pairs)  27.8 us
    ppermute x6, starting transfers between devices, passed_along(): return lax.ppermute(x, axis, pairs)  23.4 us
    gather x24, local copies, waits for them, and re-layouts  22.6 us
    ppermute x7, starting transfers between devices, padded_2(): lax.ppermute(lax.slice_in_dim(block, 0, width, axis=dim), axis, backward)  15.6 us
    ppermute x7, waiting for transfers between devices, padded_2(): lax.ppermute(lax.slice_in_dim(block, block.shape[dim] - width, None, axis...  6.45 us
    add x6, other arithmetic, solve_slabs(): potential = potential + weights[k] * (density - applied) / 6.5  5.57 us
  transfers between devices with their start and end apart: 20, of which 11 were waited for; matrix products, arithmetic and copies ran while one was open for 4% of the time, Pallas kernels for 0%

commit v1 on v0

v1 whole, which is shorter than its diff:
```python
import functools
import math

import jax
import jax.numpy as jnp
from jax import lax
from jax.experimental import pallas as pl
from jax.experimental.pallas import tpu as pltpu
from jax.sharding import PartitionSpec as P

BZ = 64
SPAN = 16
SWEEPS = 8
REACH = 4
LANES = 128
EDGE = 8
LOW = 16
CHUNKS = 8
MESH = pl.DeviceIdType.MESH


def sweep_weights():
    low = 0.5 / 6.5
    high = 12.5 / 6.5
    center = (high + low) / 2.0
    half = (high - low) / 2.0
    return [
        1.0 / (center + half * math.cos(math.pi * (2 * k + 1) / (2 * SWEEPS)))
        for k in range(SWEEPS)
    ]


def remote(src, dst, send, recv, target):
    return pltpu.make_async_remote_copy(
        src_ref=src, dst_ref=dst, send_sem=send, recv_sem=recv,
        device_id=target, device_id_type=MESH,
    )


def enter(near):
    barrier = pltpu.get_barrier_semaphore()
    for there, target in near:
        @pl.when(there)
        def _(target=target):
            pl.semaphore_signal(barrier, inc=1, device_id=target, device_id_type=MESH)
    count = jnp.int32(0)
    for there, target in near:
        count = count + jnp.where(there, 1, 0)
    pl.semaphore_wait(barrier, count)


def gather_kernel(
    wides, quads, orb, corner_in, pool, corner,
    local_sem, corner_send, corner_recv, send_two, recv_two, send_one, recv_one,
    edge_send, edge_recv, own_send, own_recv,
):
    owned, planes, flat = orb.shape
    chunk_width = flat // CHUNKS
    w = lax.axis_index("wide")
    q = lax.axis_index("quad")
    odd = lax.rem(w, 2)
    is_odd = odd == 1
    is_even = odd == 0
    pair = w + 1 - 2 * odd
    has_one = jnp.logical_or(is_even, w + 1 < wides)
    has_two = w + 2 < wides
    gives_two = w >= 2
    below = q >= 1
    above = q + 1 < quads
    enter([
        (w >= 1, {"wide": w - 1}), (gives_two, {"wide": w - 2}),
        (w + 1 < wides, {"wide": w + 1}), (has_two, {"wide": w + 2}),
        (below, {"quad": q - 1}), (above, {"quad": q + 1}),
    ])

    def columns(c):
        return pl.ds(c * chunk_width, chunk_width)

    def held(step, c):
        return pool.at[pl.ds(step * owned, owned), pl.ds(EDGE, planes), columns(c)]

    def corner_copy(step):
        return remote(
            corner_in, corner.at[step], corner_send.at[step - 1], corner_recv.at[step - 1],
            {"wide": w - step},
        )

    def own_to_two(c):
        return remote(
            orb.at[:, :, columns(c)], held(2, c), send_two.at[c], recv_two.at[c],
            {"wide": w - 2},
        )

    def own_to_pair(c):
        return remote(
            orb.at[:, :, columns(c)], held(1, c), send_one.at[c], recv_one.at[c],
            {"wide": pair},
        )

    def two_to_pair(c):
        return remote(held(2, c), held(1, c), send_one.at[c], recv_one.at[c], {"wide": pair})

    def own_edge(up):
        if up:
            return remote(
                orb.at[:, pl.ds(planes - EDGE, EDGE)],
                pool.at[pl.ds(0, owned), pl.ds(0, EDGE)],
                own_send.at[1], own_recv.at[1], {"quad": q + 1},
            )
        return remote(
            orb.at[:, pl.ds(0, EDGE)],
            pool.at[pl.ds(0, owned), pl.ds(EDGE + planes, EDGE)],
            own_send.at[0], own_recv.at[0], {"quad": q - 1},
        )

    def edge(step, up, c):
        rows = pl.ds(step * owned, owned)
        if up:
            src, dst, to = planes, 0, q + 1
        else:
            src, dst, to = EDGE, EDGE + planes, q - 1
        return remote(
            pool.at[rows, pl.ds(src, EDGE), columns(c)],
            pool.at[rows, pl.ds(dst, EDGE), columns(c)],
            edge_send.at[step - 1, int(up), c], edge_recv.at[step - 1, int(up), c],
            {"quad": to},
        )

    own_copy = pltpu.make_async_copy(
        orb, pool.at[pl.ds(0, owned), pl.ds(EDGE, planes)], local_sem.at[0]
    )
    corner_copy_own = pltpu.make_async_copy(corner_in, corner.at[0], local_sem.at[1])
    for step in (1, 2):
        @pl.when(w >= step)
        def _(step=step):
            corner_copy(step).start()
    for c in range(CHUNKS):
        @pl.when(gives_two)
        def _(c=c):
            own_to_two(c).start()

        @pl.when(is_odd)
        def _(c=c):
            own_to_pair(c).start()

    @pl.when(below)
    def _():
        own_edge(False).start()

    @pl.when(above)
    def _():
        own_edge(True).start()
    own_copy.start()
    corner_copy_own.start()

    def pass_edges(step, c):
        @pl.when(below)
        def _():
            edge(step, False, c).start()

        @pl.when(above)
        def _():
            edge(step, True, c).start()

    for c in range(CHUNKS):
        @pl.when(has_two)
        def _(c=c):
            own_to_two(c).wait_recv()

            @pl.when(is_even)
            def _():
                two_to_pair(c).start()
            pass_edges(2, c)

        @pl.when(has_one)
        def _(c=c):
            own_to_pair(c).wait_recv()
            pass_edges(1, c)

    for up, takes, gives in ((False, above, below), (True, below, above)):
        @pl.when(takes)
        def _(up=up):
            own_edge(up).wait_recv()

        @pl.when(gives)
        def _(up=up):
            own_edge(up).wait_send()
        for step, have in ((2, has_two), (1, has_one)):
            for c in range(CHUNKS):
                @pl.when(jnp.logical_and(takes, have))
                def _(up=up, step=step, c=c):
                    edge(step, up, c).wait_recv()

                @pl.when(jnp.logical_and(gives, have))
                def _(up=up, step=step, c=c):
                    edge(step, up, c).wait_send()
    for step in (1, 2):
        @pl.when(w + step < wides)
        def _(step=step):
            corner_copy(step).wait_recv()

        @pl.when(w >= step)
        def _(step=step):
            corner_copy(step).wait_send()
    for c in range(CHUNKS):
        @pl.when(gives_two)
        def _(c=c):
            own_to_two(c).wait_send()

        @pl.when(jnp.logical_or(is_odd, has_two))
        def _(c=c):
            own_to_pair(c).wait_send()
    own_copy.wait()
    corner_copy_own.wait()


def exchange_kernel(
    quads, pool, corner_s, partner_ref, live_ref, seg, dens, moved, pot, final, prod,
):
    total_orbs, wide_rows, flat = pool.shape
    owned = total_orbs // 3
    planes = wide_rows - 2 * EDGE
    slots = partner_ref.shape[0]
    tiles = flat // LANES
    rows_y = flat // BZ
    w = lax.axis_index("wide")
    q = lax.axis_index("quad")

    zero_rows = jnp.zeros((dens.shape[2], LANES), jnp.float32)
    for s in range(slots):
        dens[s, 0] = zero_rows
        dens[s, tiles + 1] = zero_rows
    for b in range(2):
        pot[b, 0] = zero_rows
        pot[b, tiles + 1] = zero_rows

    lane = lax.broadcasted_iota(jnp.int32, (wide_rows, LANES), 1)
    zpos = lax.rem(lane, BZ)
    ylow = lane // BZ
    plane = lax.broadcasted_iota(jnp.int32, (wide_rows, LANES), 0) + (q * planes - EDGE)
    in_box = (plane >= 0) & (plane < quads * planes)

    def slot_facts(s):
        left = s % owned
        right = jnp.clip(partner_ref[s] - w * owned, 0, 3 * owned - 1)
        live = live_ref[s] != 0
        who, which = right // owned, lax.rem(right, owned)
        dy = corner_s[who, which, 0] - corner_s[0, left, 0]
        dz = corner_s[who, which, 1] - corner_s[0, left, 1]
        dy = jnp.clip(jnp.where(live, dy, 0), -SPAN, SPAN)
        dz = jnp.clip(jnp.where(live, dz, 0), -SPAN, SPAN)
        return left, right, live, dy, dz

    def mover(dy, dz, ok, rows):
        by = dy * BZ + dz
        whole = by >> 7
        rest = by & (LANES - 1)
        near_part = lane[:rows] < LANES - rest
        zfrom = zpos[:rows] - dz
        keep_z = (zfrom >= 0) & (zfrom < BZ) & ok
        yfrom = ylow[:rows] - dy

        def move(load, r):
            here = load(jnp.clip(r - whole, 0, tiles - 1))
            before = load(jnp.clip(r - whole - 1, 0, tiles - 1))
            turned = pltpu.roll(jnp.where(near_part, here, before), rest, 1)
            source = yfrom + 2 * r
            keep = keep_z & (source >= 0) & (source < rows_y)
            return jnp.where(keep, turned, 0.0)

        return move

    def column(t):
        return pl.ds(pl.multiple_of(t * LANES, LANES), LANES)

    facts = [slot_facts(s) for s in range(slots)]
    for s in range(slots):
        left, right, live, dy, dz = facts[s]
        move = mover(dy, dz, live, wide_rows)

        def one_tile(r, carry, s=s, left=left, right=right, move=move):
            there = move(lambda t: pool[right, :, column(t)], r)
            moved[s, r] = there[EDGE:EDGE + planes]
            dens[s, r + 1, LOW - EDGE:LOW + planes + EDGE] = jnp.where(
                in_box, there * pool[left, :, column(r)], 0.0
            )
            return carry

        lax.fori_loop(0, tiles, one_tile, 0, unroll=2)

    weights = sweep_weights()

    def stencil(read, r, first, size):
        upper = lane[:size] >= BZ
        v = read(r + 1, first, size)
        cross = v + jnp.where(upper, read(r, first, size), read(r + 2, first, size))
        total = read(r + 1, first + 1, size) + read(r + 1, first - 1, size)
        total = total + pltpu.roll(cross, BZ, 1)
        total = total + jnp.where(zpos[:size] > 0, pltpu.roll(v, 1, 1), 0.0)
        total = total + jnp.where(zpos[:size] < BZ - 1, pltpu.roll(v, LANES - 1, 1), 0.0)
        return v, total

    def one_slot(s, carry):
        for k in range(1, SWEEPS):
            gain = weights[k] / 6.5
            if k == 1:
                read = lambda t, first, size: dens[s, t, pl.ds(first, size)]
            else:
                read = lambda t, first, size, b=k % 2: pot[b, t, pl.ds(first, size)]
            last = k == SWEEPS - 1

            def one_tile(r, inner, k=k, gain=gain, read=read, last=last):
                first, size = (LOW, planes) if last else (LOW - EDGE, wide_rows)
                v, total = stencil(read, r, first, size)
                if k == 1:
                    start = weights[0] / 6.5
                    new = ((1.0 - weights[1]) * start + gain) * v + (gain * start) * total
                else:
                    d = dens[s, r + 1, pl.ds(first, size)]
                    new = (1.0 - weights[k]) * v + gain * (d + total)
                if last:
                    final[s, r] = new
                    prod[s, r] = new * pool[lax.rem(s, owned), EDGE:EDGE + planes, column(r)]
                else:
                    pot[(k + 1) % 2, r + 1, pl.ds(first, size)] = jnp.where(in_box, new, 0.0)
                return inner

            lax.fori_loop(0, tiles, one_tile, 0, unroll=4)
        return carry

    lax.fori_loop(0, slots, one_slot, 0)

    backs = [mover(-dy, -dz, live, planes) for left, right, live, dy, dz in facts]

    def terms(r, carry):
        total = [jnp.zeros((planes, LANES), jnp.float32) for o in range(3 * owned)]
        for s in range(slots):
            left, right = facts[s][:2]
            total[left] = total[left] + final[s, r] * moved[s, r]
            term = backs[s](lambda t: prod[s, t], r)
            for o in range(left + 1, min(left + 1 + REACH, 3 * owned)):
                total[o] = total[o] + jnp.where(right == o, term, 0.0)
        for o in range(3 * owned):
            seg[o, :, column(r)] = total[o]
        return carry

    lax.fori_loop(0, tiles, terms, 0, unroll=2)


def return_kernel(
    wides, seg, out, own, two, from_pair, from_two,
    local_sem, send_one, recv_one, send_two, recv_two,
):
    owned, planes, flat = out.shape
    chunk_width = flat // CHUNKS
    w = lax.axis_index("wide")
    odd = lax.rem(w, 2)
    is_odd = odd == 1
    is_even = odd == 0
    pair = w + 1 - 2 * odd
    has_two = w + 2 < wides
    takes_two = w >= 2
    sends_pair = jnp.logical_or(is_even, w + 1 < wides)
    takes_pair = jnp.logical_or(is_odd, has_two)
    even_two = jnp.logical_and(is_even, has_two)

    own_copy = pltpu.make_async_copy(seg.at[pl.ds(0, owned)], own, local_sem.at[0])
    two_copy = pltpu.make_async_copy(seg.at[pl.ds(2 * owned, owned)], two, local_sem.at[1])
    own_copy.start()
    two_copy.start()
    enter([
        (w >= 0, {"wide": pair}), (takes_two, {"wide": w - 2}), (has_two, {"wide": w + 2}),
    ])

    def columns(c):
        return pl.ds(c * chunk_width, chunk_width)

    def back_to_pair(c):
        return remote(
            seg.at[pl.ds(owned, owned), :, columns(c)], from_pair.at[:, :, columns(c)],
            send_one.at[c], recv_one.at[c], {"wide": pair},
        )

    def back_to_two(c):
        return remote(
            two.at[:, :, columns(c)], from_two.at[:, :, columns(c)],
            send_two.at[c], recv_two.at[c], {"wide": w + 2},
        )

    for c in range(CHUNKS):
        @pl.when(sends_pair)
        def _(c=c):
            back_to_pair(c).start()
    two_copy.wait()
    for c in range(CHUNKS):
        @pl.when(jnp.logical_and(is_odd, has_two))
        def _(c=c):
            back_to_two(c).start()
    for c in range(CHUNKS):
        @pl.when(takes_pair)
        def _(c=c):
            back_to_pair(c).wait_recv()

        @pl.when(even_two)
        def _(c=c):
            two[:, :, columns(c)] += from_pair[:, :, columns(c)]
            back_to_two(c).start()
    own_copy.wait()
    for c in range(CHUNKS):
        out[:, :, columns(c)] = own[:, :, columns(c)]

        @pl.when(is_odd)
        def _(c=c):
            out[:, :, columns(c)] += from_pair[:, :, columns(c)]

        @pl.when(takes_two)
        def _(c=c):
            back_to_two(c).wait_recv()
            out[:, :, columns(c)] += from_two[:, :, columns(c)]
    for c in range(CHUNKS):
        @pl.when(sends_pair)
        def _(c=c):
            back_to_pair(c).wait_send()

        @pl.when(has_two)
        def _(c=c):
            back_to_two(c).wait_send()


def per_device(wides, quads, orbitals, corners, pair_partner, pair_live):
    owned, planes, flat = orbitals.shape
    slots = pair_partner.shape[0]
    tiles = flat // LANES
    field_rows = planes + 2 * LOW
    corner_block = jnp.zeros((8, LANES), jnp.int32).at[:owned, :2].set(corners)
    f32 = jnp.float32
    dma = pltpu.SemaphoreType.DMA
    vmem = pl.BlockSpec(memory_space=pltpu.VMEM)
    smem = pl.BlockSpec(memory_space=pltpu.SMEM)
    anywhere = pl.BlockSpec(memory_space=pl.ANY)
    limit = 32 * 1024 * 1024
    pool, pool_corner = pl.pallas_call(
        functools.partial(gather_kernel, wides, quads),
        out_shape=(
            jax.ShapeDtypeStruct((3 * owned, planes + 2 * EDGE, flat), f32),
            jax.ShapeDtypeStruct((3, 8, LANES), jnp.int32),
        ),
        in_specs=[anywhere, anywhere],
        out_specs=(anywhere, anywhere),
        scratch_shapes=[
            dma((2,)), dma((2,)), dma((2,)),
            dma((CHUNKS,)), dma((CHUNKS,)), dma((CHUNKS,)), dma((CHUNKS,)),
            dma((2, 2, CHUNKS)), dma((2, 2, CHUNKS)), dma((2,)), dma((2,)),
        ],
        compiler_params=pltpu.CompilerParams(
            collective_id=0, has_side_effects=True, vmem_limit_bytes=limit
        ),
        name="gather",
    )(orbitals, corner_block)
    seg = pl.pallas_call(
        functools.partial(exchange_kernel, quads),
        out_shape=jax.ShapeDtypeStruct((3 * owned, planes, flat), f32),
        in_specs=[vmem, smem, smem, smem],
        out_specs=vmem,
        scratch_shapes=[
            pltpu.VMEM((slots, tiles + 2, field_rows, LANES), f32),
            pltpu.VMEM((slots, tiles, planes, LANES), f32),
            pltpu.VMEM((2, tiles + 2, field_rows, LANES), f32),
            pltpu.VMEM((slots, tiles, planes, LANES), f32),
            pltpu.VMEM((slots, tiles, planes, LANES), f32),
        ],
        compiler_params=pltpu.CompilerParams(vmem_limit_bytes=limit),
        name="exchange",
    )(pool, pool_corner, pair_partner, pair_live)
    return pl.pallas_call(
        functools.partial(return_kernel, wides),
        out_shape=jax.ShapeDtypeStruct(orbitals.shape, f32),
        in_specs=[anywhere],
        out_specs=vmem,
        scratch_shapes=[
            pltpu.VMEM((owned, planes, flat), f32),
            pltpu.VMEM((owned, planes, flat), f32),
            pltpu.VMEM((owned, planes, flat), f32),
            pltpu.VMEM((owned, planes, flat), f32),
            dma((2,)), dma((CHUNKS,)), dma((CHUNKS,)), dma((CHUNKS,)), dma((CHUNKS,)),
        ],
        compiler_params=pltpu.CompilerParams(
            collective_id=1, has_side_effects=True, vmem_limit_bytes=limit
        ),
        name="give_back",
    )(seg)


def solution(mesh):
    in_specs = (P("wide", "quad", None), P("wide", None), P("wide"), P("wide"))
    out_specs = P("wide", "quad", None)
    body = functools.partial(per_device, mesh.shape["wide"], mesh.shape["quad"])
    return jax.shard_map(
        body, mesh=mesh, in_specs=in_specs, out_specs=out_specs, check_vma=False
    )
```

time: 160 us -> 78.6 us (0.49)
  the two profiles are of different devices: /device:TPU:13 before, /device:TPU:17 now
where the time goes in v1:
time: 78.6 us; the launch traced here: 78.4 us
  Pallas kernels  74.6 us (95%)
  local copies, waits for them, and re-layouts  3.83 us (5%)
    pallas_call x1, Pallas kernels, per_device(): pl.pallas_call(functools.partial(exchange_kernel, quads), out_shape=jax.S...  34.8 us
    pallas_call x1, Pallas kernels, per_device(): pl.pallas_call(functools.partial(return_kernel, wides), out_shape=jax.Sha...  20.1 us
    pallas_call x1, Pallas kernels, per_device(): pl.pallas_call(functools.partial(gather_kernel, wides, quads), out_shape=...  19.7 us
    unnamed x7, local copies, waits for them, and re-layouts  3.14 us

profile of v1, /device:TPU:17, one launch (start us, length us, event | category | flops | bytes accessed | tf_op | source)
XLA Modules:
  0.0 78.4 jit_solution(5152161096629574993)
XLA Ops:
  0.0 0.7 scatter.4.corner_in
  0.7 0.0 copy-start
  0.7 1.0 %copy-done = f32[2,16,4096]{2,1,0:T(8,128)S(1)} copy-done((f32[2,16,4096]{2,1,0:T(8,128)S(1)}, f32[2,16,4096]{2,1,0:T(8,128)}, u32[]{:S(2)}) %copy-start) | copy-done | bytes 524312
  1.7 19.7 %gather.1 = (f32[6,32,4096]{2,1,0:T(8,128)S(1)}, s32[3,8,128]{2,1,0:T(8,128)S(1)}) custom-call(f32[2,16,4096]{2,1,0:T(8,128)S(1)} %copy-done, s32[8,128]{1,0:T(8,128)S(1)} %scatter.4.corner_in), custom_call_target="tpu_custom_call" | custom-call | tf_op jit(solution)/shard_map/gather/pallas_call | solution.py:442
  21.4 0.0 copy-start.1
  21.4 0.6 copy-done.1
  22.1 0.0 copy-start.2
  22.1 0.7 copy-done.2
  22.7 34.8 %exchange.1.seg = f32[6,16,4096]{2,1,0:T(8,128)S(1)} custom-call(f32[6,32,4096]{2,1,0:T(8,128)S(1)} %get-tuple-element.19.pool, s32[3,8,128]{2,1,0:T(8,128)S(1)} %get-tuple-element.20.corner_s, s32[4]{0:T(128)S(1)} %copy-done.1, s32[4]{0:T(128)S(1)} %copy-done.2), custom_call_target="tpu_custom_call" | custom-call | tf_op jit(solution)/shard_map/exchange/pallas_call | solution.py:460
  57.6 20.1 %give_back.1 = f32[2,16,4096]{2,1,0:T(8,128)S(1)} custom-call(f32[6,16,4096]{2,1,0:T(8,128)S(1)} %exchange.1.seg), custom_call_target="tpu_custom_call" | custom-call | tf_op jit(solution)/shard_map/give_back/pallas_call | solution.py:475
  77.6 0.8 %copy.6 = f32[2,16,4096]{2,1,0:T(8,128)} copy(f32[2,16,4096]{2,1,0:T(8,128)S(1)} %give_back.1) | data formatting | bytes 1048576
Async XLA Ops:
  0.7 1.0 %copy-start = (f32[2,16,4096]{2,1,0:T(8,128)S(1)}, f32[2,16,4096]{2,1,0:T(8,128)}, u32[]{:S(2)}) copy-start(f32[2,16,4096]{2,1,0:T(8,128)} %orb.1) | copy-start | bytes 1572868
  21.4 0.7 copy-start.1
  22.1 0.7 copy-start.2

commit v2 on v1

--- a/solution.py
+++ b/solution.py
@@ -16,6 +16,8 @@
 EDGE = 8
 LOW = 16
 CHUNKS = 8
+AHEAD = 3
+GROUP = 4
 MESH = pl.DeviceIdType.MESH
 
 
@@ -134,22 +136,15 @@
         @pl.when(w >= step)
         def _(step=step):
             corner_copy(step).start()
-    for c in range(CHUNKS):
-        @pl.when(gives_two)
+    paced = jnp.logical_and(is_even, has_two)
+    for c in range(CHUNKS):
+        @pl.when(gives_two if c < AHEAD else jnp.logical_and(gives_two, jnp.logical_not(paced)))
         def _(c=c):
             own_to_two(c).start()
 
         @pl.when(is_odd)
         def _(c=c):
             own_to_pair(c).start()
-
-    @pl.when(below)
-    def _():
-        own_edge(False).start()
-
-    @pl.when(above)
-    def _():
-        own_edge(True).start()
     own_copy.start()
     corner_copy_own.start()
 
@@ -170,12 +165,25 @@
             @pl.when(is_even)
             def _():
                 two_to_pair(c).start()
+            if c + AHEAD < CHUNKS:
+                @pl.when(jnp.logical_and(is_even, gives_two))
+                def _():
+                    own_to_two(c + AHEAD).start()
             pass_edges(2, c)
 
         @pl.when(has_one)
         def _(c=c):
             own_to_pair(c).wait_recv()
             pass_edges(1, c)
+
+        if c == 0:
+            @pl.when(below)
+            def _():
+                own_edge(False).start()
+
+            @pl.when(above)
+            def _():
+                own_edge(True).start()
 
     for up, takes, gives in ((False, above, below), (True, below, above)):
         @pl.when(takes)
@@ -215,7 +223,7 @@
 
 
 def exchange_kernel(
-    quads, pool, corner_s, partner_ref, live_ref, seg, dens, moved, pot, final, prod,
+    quads, pool, corner_s, partner_ref, live_ref, seg, dens, moved, pot_a, pot_b, final, prod,
 ):
     total_orbs, wide_rows, flat = pool.shape
     owned = total_orbs // 3
@@ -230,9 +238,10 @@
     for s in range(slots):
         dens[s, 0] = zero_rows
         dens[s, tiles + 1] = zero_rows
-    for b in range(2):
-        pot[b, 0] = zero_rows
-        pot[b, tiles + 1] = zero_rows
+    pots = (pot_a, pot_b)
+    for pot in pots:
+        pot[0] = zero_rows
+        pot[tiles + 1] = zero_rows
 
     lane = lax.broadcasted_iota(jnp.int32, (wide_rows, LANES), 1)
     zpos = lax.rem(lane, BZ)
@@ -290,15 +299,12 @@
 
     weights = sweep_weights()
 
-    def stencil(read, r, first, size):
-        upper = lane[:size] >= BZ
-        v = read(r + 1, first, size)
-        cross = v + jnp.where(upper, read(r, first, size), read(r + 2, first, size))
-        total = read(r + 1, first + 1, size) + read(r + 1, first - 1, size)
-        total = total + pltpu.roll(cross, BZ, 1)
+    def stencil(v, before, after, up, down):
+        size = v.shape[0]
+        cross = v + jnp.where(lane[:size] >= BZ, before, after)
+        total = (up + down) + pltpu.roll(cross, BZ, 1)
         total = total + jnp.where(zpos[:size] > 0, pltpu.roll(v, 1, 1), 0.0)
-        total = total + jnp.where(zpos[:size] < BZ - 1, pltpu.roll(v, LANES - 1, 1), 0.0)
-        return v, total
+        return total + jnp.where(zpos[:size] < BZ - 1, pltpu.roll(v, LANES - 1, 1), 0.0)
 
     def one_slot(s, carry):
         for k in range(1, SWEEPS):
@@ -306,26 +312,38 @@
             if k == 1:
                 read = lambda t, first, size: dens[s, t, pl.ds(first, size)]
             else:
-                read = lambda t, first, size, b=k % 2: pot[b, t, pl.ds(first, size)]
+                read = lambda t, first, size, k=k: pots[k % 2][t, pl.ds(first, size)]
             last = k == SWEEPS - 1
 
-            def one_tile(r, inner, k=k, gain=gain, read=read, last=last):
+            def some_tiles(i, inner, k=k, gain=gain, read=read, last=last):
+                r = i * GROUP
                 first, size = (LOW, planes) if last else (LOW - EDGE, wide_rows)
-                v, total = stencil(read, r, first, size)
-                if k == 1:
-                    start = weights[0] / 6.5
-                    new = ((1.0 - weights[1]) * start + gain) * v + (gain * start) * total
-                else:
-                    d = dens[s, r + 1, pl.ds(first, size)]
-                    new = (1.0 - weights[k]) * v + gain * (d + total)
-                if last:
-                    final[s, r] = new
-                    prod[s, r] = new * pool[lax.rem(s, owned), EDGE:EDGE + planes, column(r)]
-                else:
-                    pot[(k + 1) % 2, r + 1, pl.ds(first, size)] = jnp.where(in_box, new, 0.0)
+                here = [read(r + g, first, size) for g in range(GROUP + 2)]
+                up = [read(r + g + 1, first + 1, size) for g in range(GROUP)]
+                down = [read(r + g + 1, first - 1, size) for g in range(GROUP)]
+                news = []
+                for g in range(GROUP):
+                    v = here[g + 1]
+                    total = stencil(v, here[g], here[g + 2], up[g], down[g])
+                    if k == 1:
+                        start = weights[0] / 6.5
+                        new = ((1.0 - weights[1]) * start + gain) * v + (gain * start) * total
+                    else:
+                        d = dens[s, r + g + 1, pl.ds(first, size)]
+                        new = (1.0 - weights[k]) * v + gain * (d + total)
+                    if not last:
+                        new = jnp.where(in_box, new, 0.0)
+                    news.append(new)
+                for g in range(GROUP):
+                    if last:
+                        final[s, r + g] = news[g]
+                        own = pool[lax.rem(s, owned), EDGE:EDGE + planes, column(r + g)]
+                        prod[s, r + g] = news[g] * own
+                    else:
+                        pots[(k + 1) % 2][r + g + 1, pl.ds(first, size)] = news[g]
                 return inner
 
-            lax.fori_loop(0, tiles, one_tile, 0, unroll=4)
+            lax.fori_loop(0, tiles // GROUP, some_tiles, 0)
         return carry
 
     lax.fori_loop(0, slots, one_slot, 0)
@@ -387,12 +405,12 @@
             send_two.at[c], recv_two.at[c], {"wide": w + 2},
         )
 
-    for c in range(CHUNKS):
-        @pl.when(sends_pair)
+    two_copy.wait()
+    for c in range(CHUNKS):
+        @pl.when(jnp.logical_and(sends_pair, jnp.logical_not(even_two)))
         def _(c=c):
             back_to_pair(c).start()
-    two_copy.wait()
-    for c in range(CHUNKS):
+
         @pl.when(jnp.logical_and(is_odd, has_two))
         def _(c=c):
             back_to_two(c).start()
@@ -405,6 +423,7 @@
         def _(c=c):
             two[:, :, columns(c)] += from_pair[:, :, columns(c)]
             back_to_two(c).start()
+            back_to_pair(c).start()
     own_copy.wait()
     for c in range(CHUNKS):
         out[:, :, columns(c)] = own[:, :, columns(c)]
@@ -465,7 +484,8 @@
         scratch_shapes=[
             pltpu.VMEM((slots, tiles + 2, field_rows, LANES), f32),
             pltpu.VMEM((slots, tiles, planes, LANES), f32),
-            pltpu.VMEM((2, tiles + 2, field_rows, LANES), f32),
+            pltpu.VMEM((tiles + 2, field_rows, LANES), f32),
+            pltpu.VMEM((tiles + 2, field_rows, LANES), f32),
             pltpu.VMEM((slots, tiles, planes, LANES), f32),
             pltpu.VMEM((slots, tiles, planes, LANES), f32),
         ],

time: 78.6 us -> 78.9 us (level)
  the two profiles are of different devices: /device:TPU:17 before, /device:TPU:13 now
where the time goes in v2:
time: 78.9 us; the launch traced here: 78.7 us
  Pallas kernels  74.9 us (95%)
  local copies, waits for them, and re-layouts  3.83 us (5%)
    pallas_call x1, Pallas kernels, per_device(): pl.pallas_call(functools.partial(exchange_kernel, quads), out_shape=jax.S...  34.9 us
    pallas_call x1, Pallas kernels, per_device(): pl.pallas_call(functools.partial(gather_kernel, wides, quads), out_shape=...  22.8 us
    pallas_call x1, Pallas kernels, per_device(): pl.pallas_call(functools.partial(return_kernel, wides), out_shape=jax.Sha...  17.2 us
    unnamed x7, local copies, waits for them, and re-layouts  3.14 us

profile of v2, /device:TPU:13, one launch (start us, length us, event | category | flops | bytes accessed | tf_op | source)
XLA Modules:
  0.0 78.7 jit_solution(18084032591961159993)
XLA Ops:
  0.0 0.7 scatter.4.corner_in
  0.7 0.0 copy-start
  0.7 1.0 %copy-done = f32[2,16,4096]{2,1,0:T(8,128)S(1)} copy-done((f32[2,16,4096]{2,1,0:T(8,128)S(1)}, f32[2,16,4096]{2,1,0:T(8,128)}, u32[]{:S(2)}) %copy-start) | copy-done | bytes 524312
  1.7 22.8 %gather.1 = (f32[6,32,4096]{2,1,0:T(8,128)S(1)}, s32[3,8,128]{2,1,0:T(8,128)S(1)}) custom-call(f32[2,16,4096]{2,1,0:T(8,128)S(1)} %copy-done, s32[8,128]{1,0:T(8,128)S(1)} %scatter.4.corner_in), custom_call_target="tpu_custom_call" | custom-call | tf_op jit(solution)/shard_map/gather/pallas_call | solution.py:461
  24.5 0.0 copy-start.1
  24.6 0.6 copy-done.1
  25.2 0.0 copy-start.2
  25.2 0.7 copy-done.2
  25.9 34.9 %exchange.1.seg = f32[6,16,4096]{2,1,0:T(8,128)S(1)} custom-call(f32[6,32,4096]{2,1,0:T(8,128)S(1)} %get-tuple-element.19.pool, s32[3,8,128]{2,1,0:T(8,128)S(1)} %get-tuple-element.20.corner_s, s32[4]{0:T(128)S(1)} %copy-done.1, s32[4]{0:T(128)S(1)} %copy-done.2), custom_call_target="tpu_custom_call" | custom-call | tf_op jit(solution)/shard_map/exchange/pallas_call | solution.py:479
  60.8 17.2 %give_back.1 = f32[2,16,4096]{2,1,0:T(8,128)S(1)} custom-call(f32[6,16,4096]{2,1,0:T(8,128)S(1)} %exchange.1.seg), custom_call_target="tpu_custom_call" | custom-call | tf_op jit(solution)/shard_map/give_back/pallas_call | solution.py:495
  77.9 0.8 %copy.6 = f32[2,16,4096]{2,1,0:T(8,128)} copy(f32[2,16,4096]{2,1,0:T(8,128)S(1)} %give_back.1) | data formatting | bytes 1048576
Async XLA Ops:
  0.7 1.0 %copy-start = (f32[2,16,4096]{2,1,0:T(8,128)S(1)}, f32[2,16,4096]{2,1,0:T(8,128)}, u32[]{:S(2)}) copy-start(f32[2,16,4096]{2,1,0:T(8,128)} %orb.1) | copy-start | bytes 1572868
  24.5 0.7 copy-start.1
  25.2 0.7 copy-start.2

commit v3 on v2

--- a/solution.py
+++ b/solution.py
@@ -3,6 +3,7 @@
 
 import jax
 import jax.numpy as jnp
+import numpy as np
 from jax import lax
 from jax.experimental import pallas as pl
 from jax.experimental.pallas import tpu as pltpu
@@ -30,6 +31,14 @@
         1.0 / (center + half * math.cos(math.pi * (2 * k + 1) / (2 * SWEEPS)))
         for k in range(SWEEPS)
     ]
+
+
+def sine_table():
+    count = np.arange(1, BZ + 1)
+    sine = np.sqrt(2.0 / (BZ + 1)) * np.sin(np.pi * np.outer(count, count) / (BZ + 1))
+    both = np.kron(np.eye(LANES // BZ), sine)
+    factor = np.tile(2.0 * np.cos(np.pi * count / (BZ + 1)), LANES // BZ)
+    return np.concatenate([both, np.tile(factor, (8, 1))]).astype(np.float32)
 
 
 def remote(src, dst, send, recv, target):
@@ -223,7 +232,7 @@
 
 
 def exchange_kernel(
-    quads, pool, corner_s, partner_ref, live_ref, seg, dens, moved, pot_a, pot_b, final, prod,
+    quads, pool, corner_s, partner_ref, live_ref, table, seg, dens, moved, pot_a, pot_b, final, prod,
 ):
     total_orbs, wide_rows, flat = pool.shape
     owned = total_orbs // 3
@@ -233,15 +242,6 @@
     rows_y = flat // BZ
     w = lax.axis_index("wide")
     q = lax.axis_index("quad")
-
-    zero_rows = jnp.zeros((dens.shape[2], LANES), jnp.float32)
-    for s in range(slots):
-        dens[s, 0] = zero_rows
-        dens[s, tiles + 1] = zero_rows
-    pots = (pot_a, pot_b)
-    for pot in pots:
-        pot[0] = zero_rows
-        pot[tiles + 1] = zero_rows
 
     lane = lax.broadcasted_iota(jnp.int32, (wide_rows, LANES), 1)
     zpos = lax.rem(lane, BZ)
@@ -282,29 +282,47 @@
     def column(t):
         return pl.ds(pl.multiple_of(t * LANES, LANES), LANES)
 
+    half = tiles // 2
+    factor = table[LANES:LANES + 8]
+
+    def transform(rows):
+        return jnp.dot(
+            rows, table[0:LANES], precision=lax.Precision.HIGHEST,
+            preferred_element_type=jnp.float32,
+        )
+
+    def regroup(a, b):
+        low = lane[:a.shape[0]] < BZ
+        return (
+            jnp.where(low, a, pltpu.roll(b, BZ, 1)), jnp.where(low, pltpu.roll(a, BZ, 1), b)
+        )
+
+    def guard(field):
+        rows = pl.ds(LOW - EDGE, wide_rows)
+        field[0, rows] = jnp.where(lane >= BZ, pltpu.roll(field[tiles, rows], BZ, 1), 0.0)
+        field[tiles + 1, rows] = jnp.where(lane < BZ, pltpu.roll(field[1, rows], BZ, 1), 0.0)
+
     facts = [slot_facts(s) for s in range(slots)]
     for s in range(slots):
         left, right, live, dy, dz = facts[s]
         move = mover(dy, dz, live, wide_rows)
 
-        def one_tile(r, carry, s=s, left=left, right=right, move=move):
-            there = move(lambda t: pool[right, :, column(t)], r)
-            moved[s, r] = there[EDGE:EDGE + planes]
-            dens[s, r + 1, LOW - EDGE:LOW + planes + EDGE] = jnp.where(
-                in_box, there * pool[left, :, column(r)], 0.0
-            )
+        def two_tiles(i, carry, s=s, left=left, right=right, move=move):
+            parts = []
+            for r in (i, i + half):
+                there = move(lambda t: pool[right, :, column(t)], r)
+                moved[s, r] = there[EDGE:EDGE + planes]
+                parts.append(jnp.where(in_box, there * pool[left, :, column(r)], 0.0))
+            waves = transform(jnp.concatenate(regroup(*parts)))
+            dens[s, 2 * i + 1, LOW - EDGE:LOW + planes + EDGE] = waves[:wide_rows]
+            dens[s, 2 * i + 2, LOW - EDGE:LOW + planes + EDGE] = waves[wide_rows:]
             return carry
 
-        lax.fori_loop(0, tiles, one_tile, 0, unroll=2)
+        lax.fori_loop(0, half, two_tiles, 0, unroll=2)
+        guard(dens.at[s])
 
     weights = sweep_weights()
-
-    def stencil(v, before, after, up, down):
-        size = v.shape[0]
-        cross = v + jnp.where(lane[:size] >= BZ, before, after)
-        total = (up + down) + pltpu.roll(cross, BZ, 1)
-        total = total + jnp.where(zpos[:size] > 0, pltpu.roll(v, 1, 1), 0.0)
-        return total + jnp.where(zpos[:size] < BZ - 1, pltpu.roll(v, LANES - 1, 1), 0.0)
+    pots = (pot_a, pot_b)
 
     def one_slot(s, carry):
         for k in range(1, SWEEPS):
@@ -315,35 +333,48 @@
                 read = lambda t, first, size, k=k: pots[k % 2][t, pl.ds(first, size)]
             last = k == SWEEPS - 1
 
-            def some_tiles(i, inner, k=k, gain=gain, read=read, last=last):
+            first, size = (LOW, planes) if last else (LOW - EDGE, wide_rows)
+            if k == 1:
+                start = weights[0] / 6.5
+                keep = (1.0 - weights[1]) * start + gain + gain * start * factor
+                gain = gain * start
+            else:
+                keep = (1.0 - weights[k]) + gain * factor
+            keep = jnp.concatenate([keep] * (size // 8))
+
+            def some_tiles(i, inner, k=k, gain=gain, read=read, last=last, keep=keep, first=first, size=size):
                 r = i * GROUP
-                first, size = (LOW, planes) if last else (LOW - EDGE, wide_rows)
                 here = [read(r + g, first, size) for g in range(GROUP + 2)]
-                up = [read(r + g + 1, first + 1, size) for g in range(GROUP)]
-                down = [read(r + g + 1, first - 1, size) for g in range(GROUP)]
                 news = []
                 for g in range(GROUP):
-                    v = here[g + 1]
-                    total = stencil(v, here[g], here[g + 2], up[g], down[g])
-                    if k == 1:
-                        start = weights[0] / 6.5
-                        new = ((1.0 - weights[1]) * start + gain) * v + (gain * start) * total
-                    else:
-                        d = dens[s, r + g + 1, pl.ds(first, size)]
-                        new = (1.0 - weights[k]) * v + gain * (d + total)
+                    total = read(r + g + 1, first + 1, size) + read(r + g + 1, first - 1, size)
+                    total = total + (here[g] + here[g + 2])
+                    if k > 1:
+                        total = total + dens[s, r + g + 1, pl.ds(first, size)]
+                    new = keep * here[g + 1] + gain * total
                     if not last:
                         new = jnp.where(in_box, new, 0.0)
                     news.append(new)
-                for g in range(GROUP):
-                    if last:
-                        final[s, r + g] = news[g]
-                        own = pool[lax.rem(s, owned), EDGE:EDGE + planes, column(r + g)]
-                        prod[s, r + g] = news[g] * own
-                    else:
+                if last:
+                    cells = transform(jnp.concatenate(news))
+                    for g in range(0, GROUP, 2):
+                        t = i * (GROUP // 2) + g // 2
+                        pair = regroup(
+                            cells[g * planes:(g + 1) * planes],
+                            cells[(g + 1) * planes:(g + 2) * planes],
+                        )
+                        for place, value in zip((t, t + half), pair):
+                            final[s, place] = value
+                            own = pool[lax.rem(s, owned), EDGE:EDGE + planes, column(place)]
+                            prod[s, place] = value * own
+                else:
+                    for g in range(GROUP):
                         pots[(k + 1) % 2][r + g + 1, pl.ds(first, size)] = news[g]
                 return inner
 
             lax.fori_loop(0, tiles // GROUP, some_tiles, 0)
+            if not last:
+                guard(pots[(k + 1) % 2])
         return carry
 
     lax.fori_loop(0, slots, one_slot, 0)
@@ -479,7 +510,7 @@
     seg = pl.pallas_call(
         functools.partial(exchange_kernel, quads),
         out_shape=jax.ShapeDtypeStruct((3 * owned, planes, flat), f32),
-        in_specs=[vmem, smem, smem, smem],
+        in_specs=[vmem, smem, smem, smem, vmem],
         out_specs=vmem,
         scratch_shapes=[
             pltpu.VMEM((slots, tiles + 2, field_rows, LANES), f32),
@@ -491,7 +522,7 @@
         ],
         compiler_params=pltpu.CompilerParams(vmem_limit_bytes=limit),
         name="exchange",
-    )(pool, pool_corner, pair_partner, pair_live)
+    )(pool, pool_corner, pair_partner, pair_live, jnp.asarray(sine_table()))
     return pl.pallas_call(
         functools.partial(return_kernel, wides),
         out_shape=jax.ShapeDtypeStruct(orbitals.shape, f32),

time: 78.9 us -> 74.3 us (0.942)
  Pallas kernels: 74.9 us -> 69.3 us
  local copies, waits for them, and re-layouts: 3.83 us -> 4.71 us
    pallas_call x1, Pallas kernels: 34.9 us -> 29.4 us  [per_device(): pl.pallas_call(functools.partial(exchange_kernel, quads), out_shape=jax.S...]
    unnamed x7 -> x9, local copies, waits for them, and re-layouts: 3.14 us -> 4.02 us
where the time goes in v3:
time: 74.3 us; the launch traced here: 74.1 us
  Pallas kernels  69.3 us (93%)
  local copies, waits for them, and re-layouts  4.71 us (6%)
    pallas_call x1, Pallas kernels, per_device(): pl.pallas_call(functools.partial(exchange_kernel, quads), out_shape=jax.S...  29.4 us
    pallas_call x1, Pallas kernels, per_device(): pl.pallas_call(functools.partial(gather_kernel, wides, quads), out_shape=...  22.8 us
    pallas_call x1, Pallas kernels, per_device(): pl.pallas_call(functools.partial(return_kernel, wides), out_shape=jax.Sha...  17.2 us
    unnamed x9, local copies, waits for them, and re-layouts  4.02 us

profile of v3, /device:TPU:13, one launch (start us, length us, event | category | flops | bytes accessed | tf_op | source)
XLA Modules:
  0.0 74.1 jit_solution(15064875643694305279)
XLA Ops:
  0.0 0.7 scatter.4.corner_in
  0.7 0.0 copy-start
  0.7 1.0 %copy-done = f32[2,16,4096]{2,1,0:T(8,128)S(1)} copy-done((f32[2,16,4096]{2,1,0:T(8,128)S(1)}, f32[2,16,4096]{2,1,0:T(8,128)}, u32[]{:S(2)}) %copy-start) | copy-done | bytes 524312
  1.7 22.8 %gather.1 = (f32[6,32,4096]{2,1,0:T(8,128)S(1)}, s32[3,8,128]{2,1,0:T(8,128)S(1)}) custom-call(f32[2,16,4096]{2,1,0:T(8,128)S(1)} %copy-done, s32[8,128]{1,0:T(8,128)S(1)} %scatter.4.corner_in), custom_call_target="tpu_custom_call" | custom-call | tf_op jit(solution)/shard_map/gather/pallas_call | solution.py:492
  24.5 0.0 copy-start.1
  24.6 0.9 %copy-done.1 = f32[136,128]{1,0:T(8,128)S(1)} copy-done((f32[136,128]{1,0:T(8,128)S(1)}, f32[136,128]{1,0:T(8,128)}, u32[]{:S(2)}) %copy-start.1) | copy-done | bytes 69656
  25.4 0.0 copy-start.2
  25.4 0.7 copy-done.2
  26.1 0.0 copy-start.3
  26.1 0.7 copy-done.3
  26.7 29.4 %exchange.1.seg = f32[6,16,4096]{2,1,0:T(8,128)S(1)} custom-call(f32[6,32,4096]{2,1,0:T(8,128)S(1)} %get-tuple-element.19.pool, s32[3,8,128]{2,1,0:T(8,128)S(1)} %get-tuple-element.20.corner_s, s32[4]{0:T(128)S(1)} %copy-done.2, s32[4]{0:T(128)S(1)} %copy-done.3, f32[136,128]{1,0:T(8,128)S(1)} %copy-done.1), custom_call_target="tpu_custom_call" | custom-call | tf_op jit(solution)/shard_map/exchange/pallas_call | solution.py:510
  56.1 17.2 %give_back.1 = f32[2,16,4096]{2,1,0:T(8,128)S(1)} custom-call(f32[6,16,4096]{2,1,0:T(8,128)S(1)} %exchange.1.seg), custom_call_target="tpu_custom_call" | custom-call | tf_op jit(solution)/shard_map/give_back/pallas_call | solution.py:526
  73.3 0.8 %copy.7 = f32[2,16,4096]{2,1,0:T(8,128)} copy(f32[2,16,4096]{2,1,0:T(8,128)S(1)} %give_back.1) | data formatting | bytes 1048576
Async XLA Ops:
  0.7 1.0 %copy-start = (f32[2,16,4096]{2,1,0:T(8,128)S(1)}, f32[2,16,4096]{2,1,0:T(8,128)}, u32[]{:S(2)}) copy-start(f32[2,16,4096]{2,1,0:T(8,128)} %orb.1) | copy-start | bytes 1572868
  24.5 0.9 %copy-start.1 = (f32[136,128]{1,0:T(8,128)S(1)}, f32[136,128]{1,0:T(8,128)}, u32[]{:S(2)}) copy-start(f32[136,128]{1,0:T(8,128)} %constant.29.clone.table) | copy-start | bytes 208900
  25.4 0.7 copy-start.2
  26.1 0.7 copy-start.3

commit v4 on v3

--- a/solution.py
+++ b/solution.py
@@ -18,6 +18,7 @@
 LOW = 16
 CHUNKS = 8
 AHEAD = 3
+BLOCK = 8
 GROUP = 4
 MESH = pl.DeviceIdType.MESH
 
@@ -232,12 +233,11 @@
 
 
 def exchange_kernel(
-    quads, pool, corner_s, partner_ref, live_ref, table, seg, dens, moved, pot_a, pot_b, final, prod,
+    quads, slots, pool, corner_s, table, seg, dens, moved, pot_a, pot_b, final, prod,
 ):
     total_orbs, wide_rows, flat = pool.shape
     owned = total_orbs // 3
     planes = wide_rows - 2 * EDGE
-    slots = partner_ref.shape[0]
     tiles = flat // LANES
     rows_y = flat // BZ
     w = lax.axis_index("wide")
@@ -251,8 +251,8 @@
 
     def slot_facts(s):
         left = s % owned
-        right = jnp.clip(partner_ref[s] - w * owned, 0, 3 * owned - 1)
-        live = live_ref[s] != 0
+        right = jnp.clip(corner_s[0, owned, s] - w * owned, 0, 3 * owned - 1)
+        live = corner_s[0, owned + 1, s] != 0
         who, which = right // owned, lax.rem(right, owned)
         dy = corner_s[who, which, 0] - corner_s[0, left, 0]
         dz = corner_s[who, which, 1] - corner_s[0, left, 1]
@@ -313,16 +313,25 @@
                 there = move(lambda t: pool[right, :, column(t)], r)
                 moved[s, r] = there[EDGE:EDGE + planes]
                 parts.append(jnp.where(in_box, there * pool[left, :, column(r)], 0.0))
-            waves = transform(jnp.concatenate(regroup(*parts)))
-            dens[s, 2 * i + 1, LOW - EDGE:LOW + planes + EDGE] = waves[:wide_rows]
-            dens[s, 2 * i + 2, LOW - EDGE:LOW + planes + EDGE] = waves[wide_rows:]
+            first, second = regroup(*parts)
+            dens[s, 2 * i + 1, LOW - EDGE:LOW + planes + EDGE] = first
+            dens[s, 2 * i + 2, LOW - EDGE:LOW + planes + EDGE] = second
             return carry
 
         lax.fori_loop(0, half, two_tiles, 0, unroll=2)
+
+        def to_waves(i, carry, s=s):
+            at = (s, pl.ds(1 + i * BLOCK, BLOCK), pl.ds(LOW - EDGE, wide_rows))
+            rows = dens[at].reshape(BLOCK * wide_rows, LANES)
+            dens[at] = transform(rows).reshape(BLOCK, wide_rows, LANES)
+            return carry
+
+        lax.fori_loop(0, tiles // BLOCK, to_waves, 0)
         guard(dens.at[s])
 
     weights = sweep_weights()
     pots = (pot_a, pot_b)
+    nothing = jnp.minimum(w, 0)
 
     def one_slot(s, carry):
         for k in range(1, SWEEPS):
@@ -344,10 +353,12 @@
 
             def some_tiles(i, inner, k=k, gain=gain, read=read, last=last, keep=keep, first=first, size=size):
                 r = i * GROUP
+                next_row = first + 1 + nothing
+                last_row = first - 1 + nothing
                 here = [read(r + g, first, size) for g in range(GROUP + 2)]
                 news = []
                 for g in range(GROUP):
-                    total = read(r + g + 1, first + 1, size) + read(r + g + 1, first - 1, size)
+                    total = read(r + g + 1, next_row, size) + read(r + g + 1, last_row, size)
                     total = total + (here[g] + here[g + 2])
                     if k > 1:
                         total = total + dens[s, r + g + 1, pl.ds(first, size)]
@@ -355,26 +366,27 @@
                     if not last:
                         new = jnp.where(in_box, new, 0.0)
                     news.append(new)
-                if last:
-                    cells = transform(jnp.concatenate(news))
-                    for g in range(0, GROUP, 2):
-                        t = i * (GROUP // 2) + g // 2
-                        pair = regroup(
-                            cells[g * planes:(g + 1) * planes],
-                            cells[(g + 1) * planes:(g + 2) * planes],
-                        )
-                        for place, value in zip((t, t + half), pair):
-                            final[s, place] = value
-                            own = pool[lax.rem(s, owned), EDGE:EDGE + planes, column(place)]
-                            prod[s, place] = value * own
-                else:
-                    for g in range(GROUP):
-                        pots[(k + 1) % 2][r + g + 1, pl.ds(first, size)] = news[g]
+                for g in range(GROUP):
+                    pots[(k + 1) % 2][r + g + 1, pl.ds(first, size)] = news[g]
                 return inner
 
             lax.fori_loop(0, tiles // GROUP, some_tiles, 0)
             if not last:
                 guard(pots[(k + 1) % 2])
+
+        def to_cells(i, inner):
+            at = (pl.ds(1 + i * BLOCK, BLOCK), pl.ds(LOW, planes))
+            rows = pots[SWEEPS % 2][at].reshape(BLOCK * planes, LANES)
+            cells = transform(rows).reshape(BLOCK, planes, LANES)
+            for g in range(0, BLOCK, 2):
+                t = i * (BLOCK // 2) + g // 2
+                for place, value in zip((t, t + half), regroup(cells[g], cells[g + 1])):
+                    final[s, place] = value
+                    own = pool[lax.rem(s, owned), EDGE:EDGE + planes, column(place)]
+                    prod[s, place] = value * own
+            return inner
+
+        lax.fori_loop(0, tiles // BLOCK, to_cells, 0)
         return carry
 
     lax.fori_loop(0, slots, one_slot, 0)
@@ -482,7 +494,9 @@
     slots = pair_partner.shape[0]
     tiles = flat // LANES
     field_rows = planes + 2 * LOW
-    corner_block = jnp.zeros((8, LANES), jnp.int32).at[:owned, :2].set(corners)
+    corner_block = jnp.pad(corners, ((0, 8 - owned), (0, LANES - corners.shape[1])))
+    for row, facts in ((owned, pair_partner), (owned + 1, pair_live)):
+        corner_block += jnp.pad(facts[None], ((row, 7 - row), (0, LANES - slots)))
     f32 = jnp.float32
     dma = pltpu.SemaphoreType.DMA
     vmem = pl.BlockSpec(memory_space=pltpu.VMEM)
@@ -508,9 +522,9 @@
         name="gather",
     )(orbitals, corner_block)
     seg = pl.pallas_call(
-        functools.partial(exchange_kernel, quads),
+        functools.partial(exchange_kernel, quads, slots),
         out_shape=jax.ShapeDtypeStruct((3 * owned, planes, flat), f32),
-        in_specs=[vmem, smem, smem, smem, vmem],
+        in_specs=[vmem, smem, vmem],
         out_specs=vmem,
         scratch_shapes=[
             pltpu.VMEM((slots, tiles + 2, field_rows, LANES), f32),
@@ -522,7 +536,7 @@
         ],
         compiler_params=pltpu.CompilerParams(vmem_limit_bytes=limit),
         name="exchange",
-    )(pool, pool_corner, pair_partner, pair_live, jnp.asarray(sine_table()))
+    )(pool, pool_corner, jnp.asarray(sine_table()))
     return pl.pallas_call(
         functools.partial(return_kernel, wides),
         out_shape=jax.ShapeDtypeStruct(orbitals.shape, f32),

time: 74.3 us -> 67.2 us (0.904)
  Pallas kernels: 69.3 us -> 63.5 us
  local copies, waits for them, and re-layouts: 4.71 us -> 2.71 us
    pallas_call x1, Pallas kernels: 29.4 us -> 23.5 us  [per_device(): pl.pallas_call(functools.partial(exchange_kernel, quads, slots), out_shap...]
    unnamed x9 -> x5, local copies, waits for them, and re-layouts: 4.02 us -> 2.71 us
where the time goes in v4:
time: 67.2 us; the launch traced here: 66.9 us
  Pallas kernels  63.5 us (94%)
  local copies, waits for them, and re-layouts  2.71 us (4%)
  other arithmetic  0.72 us (1%)
    pallas_call x1, Pallas kernels, per_device(): pl.pallas_call(functools.partial(exchange_kernel, quads, slots), out_shap...  23.5 us
    pallas_call x1, Pallas kernels, per_device(): pl.pallas_call(functools.partial(gather_kernel, wides, quads), out_shape=...  22.8 us
    pallas_call x1, Pallas kernels, per_device(): pl.pallas_call(functools.partial(return_kernel, wides), out_shape=jax.Sha...  17.1 us
    unnamed x5, local copies, waits for them, and re-layouts  2.71 us

profile of v4, /device:TPU:13, one launch (start us, length us, event | category | flops | bytes accessed | tf_op | source)
XLA Modules:
  0.0 66.9 jit_solution(1176120792960718909)
XLA Ops:
  0.0 0.7 %pad_add_fusion.corner_in = s32[8,128]{1,0:T(8,128)S(1)} fusion(s32[1,4]{1,0:T(1,128)} %bitcast.2, s32[1,4]{1,0:T(1,128)} %bitcast.3, s32[2,2]{1,0:T(2,128)} %param.6), kind=kLoop, calls=%fused_computation | loop fusion | flops 2048 | bytes 4144 | tf_op jit(solution)/shard_map/add | solution.py:499
  0.7 0.0 copy-start
  0.7 1.0 %copy-done = f32[2,16,4096]{2,1,0:T(8,128)S(1)} copy-done((f32[2,16,4096]{2,1,0:T(8,128)S(1)}, f32[2,16,4096]{2,1,0:T(8,128)}, u32[]{:S(2)}) %copy-start) | copy-done | bytes 524312
  1.8 22.8 %gather.1 = (f32[6,32,4096]{2,1,0:T(8,128)S(1)}, s32[3,8,128]{2,1,0:T(8,128)S(1)}) custom-call(f32[2,16,4096]{2,1,0:T(8,128)S(1)} %copy-done, s32[8,128]{1,0:T(8,128)S(1)} %pad_add_fusion.corner_in), custom_call_target="tpu_custom_call" | custom-call | tf_op jit(solution)/shard_map/gather/pallas_call | solution.py:506
  24.6 0.0 copy-start.1
  24.6 0.9 %copy-done.1 = f32[136,128]{1,0:T(8,128)S(1)} copy-done((f32[136,128]{1,0:T(8,128)S(1)}, f32[136,128]{1,0:T(8,128)}, u32[]{:S(2)}) %copy-start.1) | copy-done | bytes 69656
  25.5 23.5 %exchange.1.seg = f32[6,16,4096]{2,1,0:T(8,128)S(1)} custom-call(f32[6,32,4096]{2,1,0:T(8,128)S(1)} %get-tuple-element.7.pool, s32[3,8,128]{2,1,0:T(8,128)S(1)} %get-tuple-element.8.corner_s, f32[136,128]{1,0:T(8,128)S(1)} %copy-done.1), custom_call_target="tpu_custom_call" | custom-call | tf_op jit(solution)/shard_map/exchange/pallas_call | solution.py:524
  49.0 17.1 %give_back.1 = f32[2,16,4096]{2,1,0:T(8,128)S(1)} custom-call(f32[6,16,4096]{2,1,0:T(8,128)S(1)} %exchange.1.seg), custom_call_target="tpu_custom_call" | custom-call | tf_op jit(solution)/shard_map/give_back/pallas_call | solution.py:540
  66.1 0.8 %copy.7 = f32[2,16,4096]{2,1,0:T(8,128)} copy(f32[2,16,4096]{2,1,0:T(8,128)S(1)} %give_back.1) | data formatting | bytes 1048576
Async XLA Ops:
  0.7 1.0 %copy-start = (f32[2,16,4096]{2,1,0:T(8,128)S(1)}, f32[2,16,4096]{2,1,0:T(8,128)}, u32[]{:S(2)}) copy-start(f32[2,16,4096]{2,1,0:T(8,128)} %orb.1) | copy-start | bytes 1572868
  24.6 0.9 %copy-start.1 = (f32[136,128]{1,0:T(8,128)S(1)}, f32[136,128]{1,0:T(8,128)}, u32[]{:S(2)}) copy-start(f32[136,128]{1,0:T(8,128)} %constant.4.clone.table) | copy-start | bytes 208900

commit v5 on v4

--- a/solution.py
+++ b/solution.py
@@ -17,7 +17,7 @@
 EDGE = 8
 LOW = 16
 CHUNKS = 8
-AHEAD = 3
+AHEAD = 2
 BLOCK = 8
 GROUP = 4
 MESH = pl.DeviceIdType.MESH
@@ -146,15 +146,6 @@
         @pl.when(w >= step)
         def _(step=step):
             corner_copy(step).start()
-    paced = jnp.logical_and(is_even, has_two)
-    for c in range(CHUNKS):
-        @pl.when(gives_two if c < AHEAD else jnp.logical_and(gives_two, jnp.logical_not(paced)))
-        def _(c=c):
-            own_to_two(c).start()
-
-        @pl.when(is_odd)
-        def _(c=c):
-            own_to_pair(c).start()
     own_copy.start()
     corner_copy_own.start()
 
@@ -167,26 +158,25 @@
         def _():
             edge(step, True, c).start()
 
-    for c in range(CHUNKS):
-        @pl.when(has_two)
-        def _(c=c):
-            own_to_two(c).wait_recv()
-
-            @pl.when(is_even)
-            def _():
-                two_to_pair(c).start()
-            if c + AHEAD < CHUNKS:
-                @pl.when(jnp.logical_and(is_even, gives_two))
-                def _():
-                    own_to_two(c + AHEAD).start()
-            pass_edges(2, c)
-
-        @pl.when(has_one)
-        def _(c=c):
-            own_to_pair(c).wait_recv()
-            pass_edges(1, c)
-
-        if c == 0:
+    for step in range(CHUNKS + 2 * AHEAD):
+        if step < CHUNKS:
+            if step >= AHEAD:
+                @pl.when(gives_two)
+                def _(c=step - AHEAD):
+                    own_to_two(c).wait_send()
+
+                @pl.when(is_odd)
+                def _(c=step - AHEAD):
+                    own_to_pair(c).wait_send()
+
+            @pl.when(gives_two)
+            def _(c=step):
+                own_to_two(c).start()
+
+            @pl.when(is_odd)
+            def _(c=step):
+                own_to_pair(c).start()
+        if step == 0:
             @pl.when(below)
             def _():
                 own_edge(False).start()
@@ -194,6 +184,20 @@
             @pl.when(above)
             def _():
                 own_edge(True).start()
+        if 0 <= step - AHEAD < CHUNKS:
+            @pl.when(has_two)
+            def _(c=step - AHEAD):
+                own_to_two(c).wait_recv()
+
+                @pl.when(is_even)
+                def _():
+                    two_to_pair(c).start()
+                pass_edges(2, c)
+        if 0 <= step - 2 * AHEAD < CHUNKS:
+            @pl.when(has_one)
+            def _(c=step - 2 * AHEAD):
+                own_to_pair(c).wait_recv()
+                pass_edges(1, c)
 
     for up, takes, gives in ((False, above, below), (True, below, above)):
         @pl.when(takes)
@@ -221,13 +225,18 @@
         def _(step=step):
             corner_copy(step).wait_send()
     for c in range(CHUNKS):
-        @pl.when(gives_two)
-        def _(c=c):
-            own_to_two(c).wait_send()
-
-        @pl.when(jnp.logical_or(is_odd, has_two))
-        def _(c=c):
-            own_to_pair(c).wait_send()
+        if c >= CHUNKS - AHEAD:
+            @pl.when(gives_two)
+            def _(c=c):
+                own_to_two(c).wait_send()
+
+            @pl.when(is_odd)
+            def _(c=c):
+                own_to_pair(c).wait_send()
+
+        @pl.when(jnp.logical_and(is_even, has_two))
+        def _(c=c):
+            two_to_pair(c).wait_send()
     own_copy.wait()
     corner_copy_own.wait()
 
@@ -285,10 +294,18 @@
     half = tiles // 2
     factor = table[LANES:LANES + 8]
 
+    bf16, f32 = jnp.bfloat16, jnp.float32
+    fine = table[0:LANES]
+    coarse = fine.astype(bf16)
+    rest = (fine - coarse.astype(f32)).astype(bf16)
+    both = jnp.concatenate([coarse, rest], axis=1)
+
     def transform(rows):
-        return jnp.dot(
-            rows, table[0:LANES], precision=lax.Precision.HIGHEST,
-            preferred_element_type=jnp.float32,
+        high = rows.astype(bf16)
+        low = (rows - high.astype(f32)).astype(bf16)
+        total = jnp.dot(high, both, preferred_element_type=f32)
+        return total[:, :LANES] + (
+            total[:, LANES:] + jnp.dot(low, coarse, preferred_element_type=f32)
         )
 
     def regroup(a, b):
@@ -421,7 +438,6 @@
     pair = w + 1 - 2 * odd
     has_two = w + 2 < wides
     takes_two = w >= 2
-    sends_pair = jnp.logical_or(is_even, w + 1 < wides)
     takes_pair = jnp.logical_or(is_odd, has_two)
     even_two = jnp.logical_and(is_even, has_two)
 
@@ -450,13 +466,20 @@
 
     two_copy.wait()
     for c in range(CHUNKS):
-        @pl.when(jnp.logical_and(sends_pair, jnp.logical_not(even_two)))
+        if c >= AHEAD:
+            @pl.when(jnp.logical_and(is_odd, has_two))
+            def _(c=c - AHEAD):
+                back_to_pair(c).wait_send()
+                back_to_two(c).wait_send()
+
+        @pl.when(jnp.logical_and(is_odd, has_two))
         def _(c=c):
             back_to_pair(c).start()
-
-        @pl.when(jnp.logical_and(is_odd, has_two))
-        def _(c=c):
             back_to_two(c).start()
+
+        @pl.when(jnp.logical_and(is_even, jnp.logical_not(has_two)))
+        def _(c=c):
+            back_to_pair(c).start()
     for c in range(CHUNKS):
         @pl.when(takes_pair)
         def _(c=c):
@@ -480,13 +503,18 @@
             back_to_two(c).wait_recv()
             out[:, :, columns(c)] += from_two[:, :, columns(c)]
     for c in range(CHUNKS):
-        @pl.when(sends_pair)
+        @pl.when(is_even)
         def _(c=c):
             back_to_pair(c).wait_send()
 
-        @pl.when(has_two)
+        @pl.when(even_two)
         def _(c=c):
             back_to_two(c).wait_send()
+        if c >= CHUNKS - AHEAD:
+            @pl.when(jnp.logical_and(is_odd, has_two))
+            def _(c=c):
+                back_to_pair(c).wait_send()
+                back_to_two(c).wait_send()
 
 
 def per_device(wides, quads, orbitals, corners, pair_partner, pair_live):

time: 67.2 us -> 65.6 us (0.976)
  Pallas kernels: 63.5 us -> 61.9 us
    pallas_call x1, Pallas kernels: 23.5 us -> 22.1 us  [per_device(): pl.pallas_call(functools.partial(exchange_kernel, quads, slots), out_shap...]
where the time goes in v5:
time: 65.6 us; the launch traced here: 65.4 us
  Pallas kernels  61.9 us (94%)
  local copies, waits for them, and re-layouts  2.71 us (4%)
  other arithmetic  0.72 us (1%)
    pallas_call x1, Pallas kernels, per_device(): pl.pallas_call(functools.partial(gather_kernel, wides, quads), out_shape=...  22.8 us
    pallas_call x1, Pallas kernels, per_device(): pl.pallas_call(functools.partial(exchange_kernel, quads, slots), out_shap...  22.1 us
    pallas_call x1, Pallas kernels, per_device(): pl.pallas_call(functools.partial(return_kernel, wides), out_shape=jax.Sha...  17.1 us
    unnamed x5, local copies, waits for them, and re-layouts  2.71 us

profile of v5, /device:TPU:13, one launch (start us, length us, event | category | flops | bytes accessed | tf_op | source)
XLA Modules:
  0.0 65.4 jit_solution(16967038518262636337)
XLA Ops:
  0.0 0.7 %pad_add_fusion.corner_in = s32[8,128]{1,0:T(8,128)S(1)} fusion(s32[1,4]{1,0:T(1,128)} %bitcast.2, s32[1,4]{1,0:T(1,128)} %bitcast.3, s32[2,2]{1,0:T(2,128)} %param.6), kind=kLoop, calls=%fused_computation | loop fusion | flops 2048 | bytes 4144 | tf_op jit(solution)/shard_map/add | solution.py:527
  0.7 0.0 copy-start
  0.7 1.0 %copy-done = f32[2,16,4096]{2,1,0:T(8,128)S(1)} copy-done((f32[2,16,4096]{2,1,0:T(8,128)S(1)}, f32[2,16,4096]{2,1,0:T(8,128)}, u32[]{:S(2)}) %copy-start) | copy-done | bytes 524312
  1.8 22.8 %gather.1 = (f32[6,32,4096]{2,1,0:T(8,128)S(1)}, s32[3,8,128]{2,1,0:T(8,128)S(1)}) custom-call(f32[2,16,4096]{2,1,0:T(8,128)S(1)} %copy-done, s32[8,128]{1,0:T(8,128)S(1)} %pad_add_fusion.corner_in), custom_call_target="tpu_custom_call" | custom-call | tf_op jit(solution)/shard_map/gather/pallas_call | solution.py:534
  24.6 0.0 copy-start.1
  24.6 0.9 %copy-done.1 = f32[136,128]{1,0:T(8,128)S(1)} copy-done((f32[136,128]{1,0:T(8,128)S(1)}, f32[136,128]{1,0:T(8,128)}, u32[]{:S(2)}) %copy-start.1) | copy-done | bytes 69656
  25.4 22.1 %exchange.1.seg = f32[6,16,4096]{2,1,0:T(8,128)S(1)} custom-call(f32[6,32,4096]{2,1,0:T(8,128)S(1)} %get-tuple-element.7.pool, s32[3,8,128]{2,1,0:T(8,128)S(1)} %get-tuple-element.8.corner_s, f32[136,128]{1,0:T(8,128)S(1)} %copy-done.1), custom_call_target="tpu_custom_call" | custom-call | tf_op jit(solution)/shard_map/exchange/pallas_call | solution.py:552
  47.5 17.1 %give_back.1 = f32[2,16,4096]{2,1,0:T(8,128)S(1)} custom-call(f32[6,16,4096]{2,1,0:T(8,128)S(1)} %exchange.1.seg), custom_call_target="tpu_custom_call" | custom-call | tf_op jit(solution)/shard_map/give_back/pallas_call | solution.py:568
  64.6 0.8 %copy.7 = f32[2,16,4096]{2,1,0:T(8,128)} copy(f32[2,16,4096]{2,1,0:T(8,128)S(1)} %give_back.1) | data formatting | bytes 1048576
Async XLA Ops:
  0.7 1.0 %copy-start = (f32[2,16,4096]{2,1,0:T(8,128)S(1)}, f32[2,16,4096]{2,1,0:T(8,128)}, u32[]{:S(2)}) copy-start(f32[2,16,4096]{2,1,0:T(8,128)} %orb.1) | copy-start | bytes 1572868
  24.6 0.9 %copy-start.1 = (f32[136,128]{1,0:T(8,128)S(1)}, f32[136,128]{1,0:T(8,128)}, u32[]{:S(2)}) copy-start(f32[136,128]{1,0:T(8,128)} %constant.4.clone.table) | copy-start | bytes 208900

commit v6 on v5

--- a/solution.py
+++ b/solution.py
@@ -324,27 +324,38 @@
         left, right, live, dy, dz = facts[s]
         move = mover(dy, dz, live, wide_rows)
 
-        def two_tiles(i, carry, s=s, left=left, right=right, move=move):
-            parts = []
-            for r in (i, i + half):
-                there = move(lambda t: pool[right, :, column(t)], r)
-                moved[s, r] = there[EDGE:EDGE + planes]
-                parts.append(jnp.where(in_box, there * pool[left, :, column(r)], 0.0))
-            first, second = regroup(*parts)
-            dens[s, 2 * i + 1, LOW - EDGE:LOW + planes + EDGE] = first
-            dens[s, 2 * i + 2, LOW - EDGE:LOW + planes + EDGE] = second
-            return carry
-
-        lax.fori_loop(0, half, two_tiles, 0, unroll=2)
-
-        def to_waves(i, carry, s=s):
-            at = (s, pl.ds(1 + i * BLOCK, BLOCK), pl.ds(LOW - EDGE, wide_rows))
-            rows = dens[at].reshape(BLOCK * wide_rows, LANES)
-            dens[at] = transform(rows).reshape(BLOCK, wide_rows, LANES)
-            return carry
-
-        lax.fori_loop(0, tiles // BLOCK, to_waves, 0)
-        guard(dens.at[s])
+        @pl.when(live)
+        def _(s=s, left=left, right=right, move=move):
+            def two_tiles(i, carry):
+                parts = []
+                for r in (i, i + half):
+                    there = move(lambda t: pool[right, :, column(t)], r)
+                    moved[s, r] = there[EDGE:EDGE + planes]
+                    parts.append(jnp.where(in_box, there * pool[left, :, column(r)], 0.0))
+                first, second = regroup(*parts)
+                dens[s, 2 * i + 1, LOW - EDGE:LOW + planes + EDGE] = first
+                dens[s, 2 * i + 2, LOW - EDGE:LOW + planes + EDGE] = second
+                return carry
+
+            lax.fori_loop(0, half, two_tiles, 0, unroll=2)
+
+            def to_waves(i, carry):
+                at = (s, pl.ds(1 + i * BLOCK, BLOCK), pl.ds(LOW - EDGE, wide_rows))
+                rows = dens[at].reshape(BLOCK * wide_rows, LANES)
+                dens[at] = transform(rows).reshape(BLOCK, wide_rows, LANES)
+                return carry
+
+            lax.fori_loop(0, tiles // BLOCK, to_waves, 0)
+            guard(dens.at[s])
+
+        @pl.when(jnp.logical_not(live))
+        def _(s=s):
+            def clear(r, carry):
+                for field in (moved, final, prod):
+                    field[s, r] = jnp.zeros((planes, LANES), jnp.float32)
+                return carry
+
+            lax.fori_loop(0, tiles, clear, 0, unroll=4)
 
     weights = sweep_weights()
     pots = (pot_a, pot_b)
@@ -406,7 +417,13 @@
         lax.fori_loop(0, tiles // BLOCK, to_cells, 0)
         return carry
 
-    lax.fori_loop(0, slots, one_slot, 0)
+    def live_slot(s, carry):
+        @pl.when(corner_s[0, owned + 1, s] != 0)
+        def _():
+            one_slot(s, 0)
+        return carry
+
+    lax.fori_loop(0, slots, live_slot, 0)
 
     backs = [mover(-dy, -dz, live, planes) for left, right, live, dy, dz in facts]
 
@@ -537,7 +554,7 @@
             jax.ShapeDtypeStruct((3 * owned, planes + 2 * EDGE, flat), f32),
             jax.ShapeDtypeStruct((3, 8, LANES), jnp.int32),
         ),
-        in_specs=[anywhere, anywhere],
+        in_specs=[pl.BlockSpec(memory_space=pltpu.HBM), anywhere],
         out_specs=(anywhere, anywhere),
         scratch_shapes=[
             dma((2,)), dma((2,)), dma((2,)),

time: 65.6 us -> 65.2 us (level); the launches traced: 65.4 us -> 64 us
  Pallas kernels: 61.9 us -> 60.5 us
    pallas_call x1, Pallas kernels: 17.1 us -> 15.6 us  [per_device(): pl.pallas_call(functools.partial(return_kernel, wides), out_shape=jax.Sha...]
where the time goes in v6:
time: 65.2 us; the launch traced here: 64 us
  Pallas kernels  60.5 us (93%)
  local copies, waits for them, and re-layouts  2.71 us (4%)
  other arithmetic  0.72 us (1%)
    pallas_call x1, Pallas kernels, per_device(): pl.pallas_call(functools.partial(gather_kernel, wides, quads), out_shape=...  22.8 us
    pallas_call x1, Pallas kernels, per_device(): pl.pallas_call(functools.partial(exchange_kernel, quads, slots), out_shap...  22.1 us
    pallas_call x1, Pallas kernels, per_device(): pl.pallas_call(functools.partial(return_kernel, wides), out_shape=jax.Sha...  15.6 us
    unnamed x5, local copies, waits for them, and re-layouts  2.71 us

profile of v6, /device:TPU:13, one launch (start us, length us, event | category | flops | bytes accessed | tf_op | source)
XLA Modules:
  0.0 64.0 jit_solution(9216752601225656867)
XLA Ops:
  0.0 0.7 %pad_add_fusion.corner_in = s32[8,128]{1,0:T(8,128)S(1)} fusion(s32[1,4]{1,0:T(1,128)} %bitcast.2, s32[1,4]{1,0:T(1,128)} %bitcast.3, s32[2,2]{1,0:T(2,128)} %param.6), kind=kLoop, calls=%fused_computation | loop fusion | flops 2048 | bytes 4144 | tf_op jit(solution)/shard_map/add | solution.py:544
  0.7 0.0 copy-start
  0.7 1.0 %copy-done = f32[2,16,4096]{2,1,0:T(8,128)S(1)} copy-done((f32[2,16,4096]{2,1,0:T(8,128)S(1)}, f32[2,16,4096]{2,1,0:T(8,128)}, u32[]{:S(2)}) %copy-start) | copy-done | bytes 524312
  1.8 22.8 %gather.1 = (f32[6,32,4096]{2,1,0:T(8,128)S(1)}, s32[3,8,128]{2,1,0:T(8,128)S(1)}) custom-call(f32[2,16,4096]{2,1,0:T(8,128)S(1)} %copy-done, s32[8,128]{1,0:T(8,128)S(1)} %pad_add_fusion.corner_in), custom_call_target="tpu_custom_call" | custom-call | tf_op jit(solution)/shard_map/gather/pallas_call | solution.py:551
  24.6 0.0 copy-start.1
  24.6 0.9 %copy-done.1 = f32[136,128]{1,0:T(8,128)S(1)} copy-done((f32[136,128]{1,0:T(8,128)S(1)}, f32[136,128]{1,0:T(8,128)}, u32[]{:S(2)}) %copy-start.1) | copy-done | bytes 69656
  25.4 22.1 %exchange.1.seg = f32[6,16,4096]{2,1,0:T(8,128)S(1)} custom-call(f32[6,32,4096]{2,1,0:T(8,128)S(1)} %get-tuple-element.7.pool, s32[3,8,128]{2,1,0:T(8,128)S(1)} %get-tuple-element.8.corner_s, f32[136,128]{1,0:T(8,128)S(1)} %copy-done.1), custom_call_target="tpu_custom_call" | custom-call | tf_op jit(solution)/shard_map/exchange/pallas_call | solution.py:569
  47.6 15.6 %give_back.1 = f32[2,16,4096]{2,1,0:T(8,128)S(1)} custom-call(f32[6,16,4096]{2,1,0:T(8,128)S(1)} %exchange.1.seg), custom_call_target="tpu_custom_call" | custom-call | tf_op jit(solution)/shard_map/give_back/pallas_call | solution.py:585
  63.2 0.8 %copy.7 = f32[2,16,4096]{2,1,0:T(8,128)} copy(f32[2,16,4096]{2,1,0:T(8,128)S(1)} %give_back.1) | data formatting | bytes 1048576
Async XLA Ops:
  0.7 1.0 %copy-start = (f32[2,16,4096]{2,1,0:T(8,128)S(1)}, f32[2,16,4096]{2,1,0:T(8,128)}, u32[]{:S(2)}) copy-start(f32[2,16,4096]{2,1,0:T(8,128)} %orb.1) | copy-start | bytes 1572868
  24.6 0.9 %copy-start.1 = (f32[136,128]{1,0:T(8,128)S(1)}, f32[136,128]{1,0:T(8,128)}, u32[]{:S(2)}) copy-start(f32[136,128]{1,0:T(8,128)} %constant.4.clone.table) | copy-start | bytes 208900

commit v7 on v6

--- a/solution.py
+++ b/solution.py
@@ -337,7 +337,7 @@
                 dens[s, 2 * i + 2, LOW - EDGE:LOW + planes + EDGE] = second
                 return carry
 
-            lax.fori_loop(0, half, two_tiles, 0, unroll=2)
+            lax.fori_loop(0, half, two_tiles, 0, unroll=4)
 
             def to_waves(i, carry):
                 at = (s, pl.ds(1 + i * BLOCK, BLOCK), pl.ds(LOW - EDGE, wide_rows))
@@ -398,7 +398,7 @@
                     pots[(k + 1) % 2][r + g + 1, pl.ds(first, size)] = news[g]
                 return inner
 
-            lax.fori_loop(0, tiles // GROUP, some_tiles, 0)
+            lax.fori_loop(0, tiles // GROUP, some_tiles, 0, unroll=2)
             if not last:
                 guard(pots[(k + 1) % 2])
 
@@ -439,7 +439,7 @@
             seg[o, :, column(r)] = total[o]
         return carry
 
-    lax.fori_loop(0, tiles, terms, 0, unroll=2)
+    lax.fori_loop(0, tiles, terms, 0, unroll=4)
 
 
 def return_kernel(

time: 65.2 us -> 62.2 us (0.954); the launches traced: 64 us -> 61.9 us
  Pallas kernels: 60.5 us -> 58.5 us
    pallas_call x1, Pallas kernels: 22.1 us -> 10.4 us  [per_device(): pl.pallas_call(functools.partial(exchange_kernel, quads, slots), out_shap...]
    pallas_call x1, Pallas kernels: 15.6 us -> 25.2 us  [per_device(): pl.pallas_call(functools.partial(return_kernel, wides), out_shape=jax.Sha...]
where the time goes in v7:
time: 62.2 us; the launch traced here: 61.9 us
  Pallas kernels  58.5 us (94%)
  local copies, waits for them, and re-layouts  2.71 us (4%)
  other arithmetic  0.72 us (1%)
    pallas_call x1, Pallas kernels, per_device(): pl.pallas_call(functools.partial(return_kernel, wides), out_shape=jax.Sha...  25.2 us
    pallas_call x1, Pallas kernels, per_device(): pl.pallas_call(functools.partial(gather_kernel, wides, quads), out_shape=...  22.8 us
    pallas_call x1, Pallas kernels, per_device(): pl.pallas_call(functools.partial(exchange_kernel, quads, slots), out_shap...  10.4 us
    unnamed x5, local copies, waits for them, and re-layouts  2.71 us

profile of v7, /device:TPU:13, one launch (start us, length us, event | category | flops | bytes accessed | tf_op | source)
XLA Modules:
  0.0 61.9 jit_solution(5690682389653475765)
XLA Ops:
  0.0 0.7 %pad_add_fusion.corner_in = s32[8,128]{1,0:T(8,128)S(1)} fusion(s32[1,4]{1,0:T(1,128)} %bitcast.2, s32[1,4]{1,0:T(1,128)} %bitcast.3, s32[2,2]{1,0:T(2,128)} %param.6), kind=kLoop, calls=%fused_computation | loop fusion | flops 2048 | bytes 4144 | tf_op jit(solution)/shard_map/add | solution.py:544
  0.7 0.0 copy-start
  0.7 1.0 %copy-done = f32[2,16,4096]{2,1,0:T(8,128)S(1)} copy-done((f32[2,16,4096]{2,1,0:T(8,128)S(1)}, f32[2,16,4096]{2,1,0:T(8,128)}, u32[]{:S(2)}) %copy-start) | copy-done | bytes 524312
  1.8 22.8 %gather.1 = (f32[6,32,4096]{2,1,0:T(8,128)S(1)}, s32[3,8,128]{2,1,0:T(8,128)S(1)}) custom-call(f32[2,16,4096]{2,1,0:T(8,128)S(1)} %copy-done, s32[8,128]{1,0:T(8,128)S(1)} %pad_add_fusion.corner_in), custom_call_target="tpu_custom_call" | custom-call | tf_op jit(solution)/shard_map/gather/pallas_call | solution.py:551
  24.6 0.0 copy-start.1
  24.6 0.9 %copy-done.1 = f32[136,128]{1,0:T(8,128)S(1)} copy-done((f32[136,128]{1,0:T(8,128)S(1)}, f32[136,128]{1,0:T(8,128)}, u32[]{:S(2)}) %copy-start.1) | copy-done | bytes 69656
  25.4 10.4 %exchange.1.seg = f32[6,16,4096]{2,1,0:T(8,128)S(1)} custom-call(f32[6,32,4096]{2,1,0:T(8,128)S(1)} %get-tuple-element.7.pool, s32[3,8,128]{2,1,0:T(8,128)S(1)} %get-tuple-element.8.corner_s, f32[136,128]{1,0:T(8,128)S(1)} %copy-done.1), custom_call_target="tpu_custom_call" | custom-call | tf_op jit(solution)/shard_map/exchange/pallas_call | solution.py:569
  35.9 25.2 %give_back.1 = f32[2,16,4096]{2,1,0:T(8,128)S(1)} custom-call(f32[6,16,4096]{2,1,0:T(8,128)S(1)} %exchange.1.seg), custom_call_target="tpu_custom_call" | custom-call | tf_op jit(solution)/shard_map/give_back/pallas_call | solution.py:585
  61.1 0.8 %copy.7 = f32[2,16,4096]{2,1,0:T(8,128)} copy(f32[2,16,4096]{2,1,0:T(8,128)S(1)} %give_back.1) | data formatting | bytes 1048576
Async XLA Ops:
  0.7 1.0 %copy-start = (f32[2,16,4096]{2,1,0:T(8,128)S(1)}, f32[2,16,4096]{2,1,0:T(8,128)}, u32[]{:S(2)}) copy-start(f32[2,16,4096]{2,1,0:T(8,128)} %orb.1) | copy-start | bytes 1572868
  24.6 0.9 %copy-start.1 = (f32[136,128]{1,0:T(8,128)S(1)}, f32[136,128]{1,0:T(8,128)}, u32[]{:S(2)}) copy-start(f32[136,128]{1,0:T(8,128)} %constant.4.clone.table) | copy-start | bytes 208900
